TPU v7x, 768 devices: a whole 4x8x12 slice. The times are simulated.
768 devices in a mesh: blk: 96 (over z, y), rep: 2 (over core), slab: 4 (over x).
Axes of the slice: x: 4, y: 8, z: 12, core: 2. Of those that a mesh axis runs over, the one named last changes fastest.
Arguments:
- t2_source: bfloat16 [2304, 128, 5120], P('blk', None, ('rep', 'slab')), may hold values from -6 to 6
- integrals: bfloat16 [8, 5120, 320], P(None, ('rep', 'slab')), may hold values from -0.078125 to 0.078125
- sector_tiles: int32 [8], replicated, may hold values from 1 to 384, 1536 in all
- block_offsets: int32 [96, 2], replicated, may hold values from 0 to 1536, as said below
Outputs:
- cycle_residual: bfloat16 [1536, 128, 320], P('blk', None, ('rep', 'slab'))
Inputs may be any that keep to these rules, and one draw needn't show every extreme that they name: `sector_tiles`: each of the 8 entries is at least 1, they sum to 1536, and one equals 384. block_offsets[0, 0] = 0, block_offsets[d, 1] = block_offsets[d + 1, 0], block_offsets[96 - 1, 1] = 1536; every boundary block_offsets[d, 0] lies within 4 of d * 16; some blk index holds exactly 24 blocks.
All inputs are finite; a program needn't handle non-finite values.
Results may differ from a plain program's by a relative error of at most 0.017.
Values may be sent and summed in bfloat16 or wider, within the bound.
No kernel may reach another device: no remote copies, remote signals or barrier semaphores. Data moves between devices by JAX's collectives and lax.ppermute only.
A program may use at most 32 MiB of HBM per device.

v0:
```python
import jax
import jax.numpy as jnp
from jax import lax
from jax.sharding import PartitionSpec as P

BLK_DEV = 16
SHIFT_MOST = 4


def from_behind(block, axis, distance):
    devices = range(lax.axis_size(axis))
    route = [(i - distance, i) for i in devices if i - distance in devices]
    return lax.ppermute(block, axis, route)


def sector_lookup(blocks, sector_tiles):
    sector_ends = jnp.cumsum(sector_tiles)
    sectors = jnp.sum((sector_ends[None, :] <= blocks[:, None]).astype(jnp.int32), axis=1)
    return jnp.minimum(sectors, sector_tiles.shape[0] - 1)


def contract(amplitudes, blocks, sector_tiles, integrals):
    sectors = sector_lookup(blocks, sector_tiles)

    def one_block(pair):
        amplitude_tile, sector = pair
        weights = lax.dynamic_index_in_dim(integrals, sector, 0, keepdims=False)
        return jnp.dot(amplitude_tile, weights, preferred_element_type=jnp.float32)

    return lax.map(one_block, (amplitudes, sectors))


def upper_start(block_offsets, device_index, slot_count):
    first_block = block_offsets[device_index, 0]
    return jnp.minimum((device_index + 1) * BLK_DEV - first_block, slot_count - SHIFT_MOST)


def outgoing(blocks_held, block_offsets, device_index):
    slot_count = blocks_held.shape[0]
    leftward = blocks_held[:SHIFT_MOST]
    start_slot = upper_start(block_offsets, device_index, slot_count)
    rightward = lax.dynamic_slice_in_dim(blocks_held, start_slot, SHIFT_MOST, 0)
    return (leftward, rightward)


def assemble(blocks_held, from_left, from_right, block_offsets, device_index, device_count):
    slot_count = blocks_held.shape[0]
    target_blocks = device_index * BLK_DEV + jnp.arange(BLK_DEV, dtype=jnp.int32)
    first_block = block_offsets[device_index, 0]
    end_block = block_offsets[device_index, 1]
    left_index = jnp.maximum(device_index - 1, 0)
    right_index = jnp.minimum(device_index + 1, device_count - 1)
    left_first = block_offsets[left_index, 0]
    left_upper = upper_start(block_offsets, left_index, slot_count)
    right_first = block_offsets[right_index, 0]
    own_slots = SHIFT_MOST + jnp.clip(target_blocks - first_block, 0, slot_count - 1)
    left_slots = jnp.clip(target_blocks - left_first - left_upper, 0, SHIFT_MOST - 1)
    right_slots = SHIFT_MOST + slot_count + jnp.clip(target_blocks - right_first, 0, SHIFT_MOST - 1)
    picked = jnp.where(
        target_blocks < first_block,
        left_slots,
        jnp.where(target_blocks >= end_block, right_slots, own_slots),
    )
    joined = jnp.concatenate([from_left, blocks_held, from_right], axis=0)
    return jnp.take(joined, picked, axis=0)


def per_device(t2_source, integrals, sector_tiles, block_offsets):
    device_index = lax.axis_index("blk")
    device_count = lax.axis_size("blk")
    leftward, rightward = outgoing(t2_source, block_offsets, device_index)
    arrived = []
    for offset, outbound in ((1, rightward), (-1, leftward)):
        arrived.append(from_behind(outbound, "blk", offset))
    target_tiles = assemble(
        t2_source, arrived[0], arrived[1], block_offsets, device_index, device_count
    )
    target_blocks = device_index * BLK_DEV + jnp.arange(BLK_DEV, dtype=jnp.int32)
    partial_value = contract(target_tiles, target_blocks, sector_tiles, integrals)
    return lax.psum_scatter(
        partial_value.astype(jnp.bfloat16), ("rep", "slab"), scatter_dimension=2, tiled=True
    )


def solution(mesh):
    in_specs = (P("blk", None, ("rep", "slab")), P(None, ("rep", "slab"), None), P(), P())
    out_specs = P("blk", None, ("rep", "slab"))
    return jax.shard_map(
        per_device, mesh=mesh, in_specs=in_specs, out_specs=out_specs, check_vma=False
    )
```

profile of v0, /device:TPU:1, one launch (start us, length us, event | category | flops | bytes accessed | tf_op | source)
XLA Modules:
  0.0 178.3 jit_solution(2286111617923916577)
XLA Ops:
  6.5 0.0 copy-start
  6.5 0.0 reduce-scatter.4.cloned.1.call-start
  6.5 1.5 constant_dynamic-slice_fusion.2
  8.7 1.4 constant_dynamic-slice_fusion
  10.1 4.1 %collective-permute-start = (bf16[4,128,640]{2,1,0:T(8,128)(2,1)S(1)}, bf16[4,128,640]{2,1,0:T(8,128)(2,1)S(1)}, u32[]{:S(2)}, u32[]{:S(2)}) collective-permute-start(bf16[4,128,640]{2,1,0:T(8,128)(2,1)S(1)} %get-tuple-element.43), channel_id=1, source_target_pairs={{0,8},{8,16},{16,24},{24,32},{32,40},{40,48},{48,56},{56,64},{64,7... | collective-permute-start | bytes 1966088 | tf_op jit(solution)/shard_map/ppermute | solution.py:13
  14.2 1.3 collective-permute-start.1
  16.0 0.0 copy-done
  16.0 0.2 reduce-window.8
  16.2 2.4 %fusion.6 = s32[16]{0:T(128)S(1)} fusion(s32[]{:T(128)} %bitcast.7, s32[]{:T(128)} %bitcast.6, s32[]{:T(128)S(6)} %min.40, s32[]{:T(128)} %bitcast.5, s32[]{:T(128)} %bitcast.4, s32[]{:T(128)S(6)} %mul.10), kind=kLoop, calls=%fused_computation.24 | loop fusion | flops 272 | bytes 88 | tf_op jit(solution)/shard_map/jit(_take)/jit(_where)/select_n | solution.py:65
  18.7 2.4 %compare_and_fusion = pred[16]{0:T(512)(128)(4,1)S(1)} fusion(s32[]{:T(128)} %bitcast.7, s32[]{:T(128)} %bitcast.6, s32[]{:T(128)S(6)} %min.40, s32[]{:T(128)} %bitcast.5, s32[]{:T(128)} %bitcast.4, s32[]{:T(128)S(6)} %mul.10), kind=kLoop, calls=%fused_computation.17 | loop fusion | flops 320 | bytes 40 | tf_op jit(solution)/shard_map/jit(_take)/and | solution.py:65
  21.1 0.1 convert_reduce_fusion
  21.2 0.4 collective-permute-done
  21.6 3.9 %collective-permute-done.1 = bf16[4,128,640]{2,1,0:T(8,128)(2,1)S(1)} collective-permute-done((bf16[4,128,640]{2,1,0:T(8,128)(2,1)S(1)}, bf16[4,128,640]{2,1,0:T(8,128)(2,1)S(1)}, u32[]{:S(2)}, u32[]{:S(2)}) %collective-permute-start.1) | collective-permute-done | bytes 655392 | tf_op jit(solution)/shard_map/ppermute | solution.py:13
  25.5 5.1 %pad_maximum_fusion = bf16[32,128,640]{2,1,0:T(8,128)(2,1)} fusion(bf16[4,128,640]{2,1,0:T(8,128)(2,1)S(1)} %collective-permute-done.1, bf16[24,128,640]{2,1,0:T(8,128)(2,1)} %param.6, bf16[4,128,640]{2,1,0:T(8,128)(2,1)S(1)} %collective-permute-done), kind=kLoop, calls=%fused_computation.8 | loop fusion | flops 5242880 | bytes 10485760 | tf_op jit(solution)/shard_map/concatenate | solution.py:64
  30.6 3.5 %gather_fusion = bf16[16,128,640]{2,1,0:T(8,128)(2,1)S(1)} fusion(bf16[32,128,640]{2,1,0:T(8,128)(2,1)} %pad_maximum_fusion, s32[1024]{0:T(1024)S(1)} %pad_clamp_fusion), kind=kCustom, calls=%fused_computation | custom fusion | bytes 5242944 | tf_op jit(solution)/shard_map/jit(_take)/gather | solution.py:65
  34.1 1.9 %broadcast_select_fusion = bf16[16,128,640]{2,1,0:T(8,128)(2,1)} fusion(bf16[16,128,640]{2,1,0:T(8,128)(2,1)S(1)} %gather_fusion, pred[16]{0:T(512)(128)(4,1)S(1)} %compare_and_fusion), kind=kLoop, calls=%fused_computation.9 | loop fusion | flops 1310720 | bytes 5242896 | tf_op jit(solution)/shard_map/jit(_take)/select_n | solution.py:65
  36.0 72.9 %while.10 = (s32[]{:T(128)}, bf16[16,128,320]{1,2,0:T(8,128)(2,1)}, bf16[16,128,640]{2,1,0:T(8,128)(2,1)}, s32[16]{0:T(128)S(1)}, bf16[8,640,320]{1,2,0:T(8,128)(2,1)}, /*index=5*/s32[]{:T(128)}, s32[]{:T(128)}, s32[]{:T(128)}) while((s32[]{:T(128)}, bf16[16,128,320]{1,2,0:T(8,128)(2,1)}, bf16[16,128,640]{2,1,0:T(8,128)(2,1)}, ...), condition=%wide.region_3.4_spmd, body=%wide.region_2.3_spmd.sunk | while | flops 52428804 | bytes 738439 | solution.py:30
  36.0 0.6 dynamic_slice.52
  38.5 2.0 %fusion.12 = bf16[16,128,320]{1,2,0:T(8,128)(2,1)} fusion(bf16[16,128,320]{1,2,0:T(8,128)(2,1)} %get-tuple-element.89, s32[]{:T(128)} %get-tuple-element.88, bf16[8,640,320]{1,2,0:T(8,128)(2,1)} %get-tuple-element.100, s32[]{:T(128)S(6)} %select_n.103, bf16[16,128,640]{2,1,0:T(8,128)(2,1)} %get-tuple-element.98), kind=kOutput, calls=%fused_computation.2.clone.1 | convolution fusion | flops 52428800 | bytes 738308 | tf_op jit(solution)/shard_map/while/body/eval_jaxpr/dot_general | solution.py:28
  40.5 0.6 dynamic_slice.52
  43.1 2.0 %fusion.12 = bf16[16,128,320]{1,2,0:T(8,128)(2,1)} fusion(bf16[16,128,320]{1,2,0:T(8,128)(2,1)} %get-tuple-element.89, s32[]{:T(128)} %get-tuple-element.88, bf16[8,640,320]{1,2,0:T(8,128)(2,1)} %get-tuple-element.100, s32[]{:T(128)S(6)} %select_n.103, bf16[16,128,640]{2,1,0:T(8,128)(2,1)} %get-tuple-element.98), kind=kOutput, calls=%fused_computation.2.clone.1 | convolution fusion | flops 52428800 | bytes 738308 | tf_op jit(solution)/shard_map/while/body/eval_jaxpr/dot_general | solution.py:28
  45.1 0.6 dynamic_slice.52
  47.7 2.0 %fusion.12 = bf16[16,128,320]{1,2,0:T(8,128)(2,1)} fusion(bf16[16,128,320]{1,2,0:T(8,128)(2,1)} %get-tuple-element.89, s32[]{:T(128)} %get-tuple-element.88, bf16[8,640,320]{1,2,0:T(8,128)(2,1)} %get-tuple-element.100, s32[]{:T(128)S(6)} %select_n.103, bf16[16,128,640]{2,1,0:T(8,128)(2,1)} %get-tuple-element.98), kind=kOutput, calls=%fused_computation.2.clone.1 | convolution fusion | flops 52428800 | bytes 738308 | tf_op jit(solution)/shard_map/while/body/eval_jaxpr/dot_general | solution.py:28
  49.6 0.6 dynamic_slice.52
  52.2 2.0 %fusion.12 = bf16[16,128,320]{1,2,0:T(8,128)(2,1)} fusion(bf16[16,128,320]{1,2,0:T(8,128)(2,1)} %get-tuple-element.89, s32[]{:T(128)} %get-tuple-element.88, bf16[8,640,320]{1,2,0:T(8,128)(2,1)} %get-tuple-element.100, s32[]{:T(128)S(6)} %select_n.103, bf16[16,128,640]{2,1,0:T(8,128)(2,1)} %get-tuple-element.98), kind=kOutput, calls=%fused_computation.2.clone.1 | convolution fusion | flops 52428800 | bytes 738308 | tf_op jit(solution)/shard_map/while/body/eval_jaxpr/dot_general | solution.py:28
  54.2 0.6 dynamic_slice.52
  56.8 2.0 %fusion.12 = bf16[16,128,320]{1,2,0:T(8,128)(2,1)} fusion(bf16[16,128,320]{1,2,0:T(8,128)(2,1)} %get-tuple-element.89, s32[]{:T(128)} %get-tuple-element.88, bf16[8,640,320]{1,2,0:T(8,128)(2,1)} %get-tuple-element.100, s32[]{:T(128)S(6)} %select_n.103, bf16[16,128,640]{2,1,0:T(8,128)(2,1)} %get-tuple-element.98), kind=kOutput, calls=%fused_computation.2.clone.1 | convolution fusion | flops 52428800 | bytes 738308 | tf_op jit(solution)/shard_map/while/body/eval_jaxpr/dot_general | solution.py:28
  58.8 0.6 dynamic_slice.52
  61.3 2.0 %fusion.12 = bf16[16,128,320]{1,2,0:T(8,128)(2,1)} fusion(bf16[16,128,320]{1,2,0:T(8,128)(2,1)} %get-tuple-element.89, s32[]{:T(128)} %get-tuple-element.88, bf16[8,640,320]{1,2,0:T(8,128)(2,1)} %get-tuple-element.100, s32[]{:T(128)S(6)} %select_n.103, bf16[16,128,640]{2,1,0:T(8,128)(2,1)} %get-tuple-element.98), kind=kOutput, calls=%fused_computation.2.clone.1 | convolution fusion | flops 52428800 | bytes 738308 | tf_op jit(solution)/shard_map/while/body/eval_jaxpr/dot_general | solution.py:28
  63.3 0.6 dynamic_slice.52
  65.9 2.0 %fusion.12 = bf16[16,128,320]{1,2,0:T(8,128)(2,1)} fusion(bf16[16,128,320]{1,2,0:T(8,128)(2,1)} %get-tuple-element.89, s32[]{:T(128)} %get-tuple-element.88, bf16[8,640,320]{1,2,0:T(8,128)(2,1)} %get-tuple-element.100, s32[]{:T(128)S(6)} %select_n.103, bf16[16,128,640]{2,1,0:T(8,128)(2,1)} %get-tuple-element.98), kind=kOutput, calls=%fused_computation.2.clone.1 | convolution fusion | flops 52428800 | bytes 738308 | tf_op jit(solution)/shard_map/while/body/eval_jaxpr/dot_general | solution.py:28
  67.9 0.6 dynamic_slice.52
  70.4 2.0 %fusion.12 = bf16[16,128,320]{1,2,0:T(8,128)(2,1)} fusion(bf16[16,128,320]{1,2,0:T(8,128)(2,1)} %get-tuple-element.89, s32[]{:T(128)} %get-tuple-element.88, bf16[8,640,320]{1,2,0:T(8,128)(2,1)} %get-tuple-element.100, s32[]{:T(128)S(6)} %select_n.103, bf16[16,128,640]{2,1,0:T(8,128)(2,1)} %get-tuple-element.98), kind=kOutput, calls=%fused_computation.2.clone.1 | convolution fusion | flops 52428800 | bytes 738308 | tf_op jit(solution)/shard_map/while/body/eval_jaxpr/dot_general | solution.py:28
  72.5 0.6 dynamic_slice.52
  75.0 2.0 %fusion.12 = bf16[16,128,320]{1,2,0:T(8,128)(2,1)} fusion(bf16[16,128,320]{1,2,0:T(8,128)(2,1)} %get-tuple-element.89, s32[]{:T(128)} %get-tuple-element.88, bf16[8,640,320]{1,2,0:T(8,128)(2,1)} %get-tuple-element.100, s32[]{:T(128)S(6)} %select_n.103, bf16[16,128,640]{2,1,0:T(8,128)(2,1)} %get-tuple-element.98), kind=kOutput, calls=%fused_computation.2.clone.1 | convolution fusion | flops 52428800 | bytes 738308 | tf_op jit(solution)/shard_map/while/body/eval_jaxpr/dot_general | solution.py:28
  77.0 0.6 dynamic_slice.52
  79.6 2.0 %fusion.12 = bf16[16,128,320]{1,2,0:T(8,128)(2,1)} fusion(bf16[16,128,320]{1,2,0:T(8,128)(2,1)} %get-tuple-element.89, s32[]{:T(128)} %get-tuple-element.88, bf16[8,640,320]{1,2,0:T(8,128)(2,1)} %get-tuple-element.100, s32[]{:T(128)S(6)} %select_n.103, bf16[16,128,640]{2,1,0:T(8,128)(2,1)} %get-tuple-element.98), kind=kOutput, calls=%fused_computation.2.clone.1 | convolution fusion | flops 52428800 | bytes 738308 | tf_op jit(solution)/shard_map/while/body/eval_jaxpr/dot_general | solution.py:28
  81.6 0.6 dynamic_slice.52
  84.1 2.0 %fusion.12 = bf16[16,128,320]{1,2,0:T(8,128)(2,1)} fusion(bf16[16,128,320]{1,2,0:T(8,128)(2,1)} %get-tuple-element.89, s32[]{:T(128)} %get-tuple-element.88, bf16[8,640,320]{1,2,0:T(8,128)(2,1)} %get-tuple-element.100, s32[]{:T(128)S(6)} %select_n.103, bf16[16,128,640]{2,1,0:T(8,128)(2,1)} %get-tuple-element.98), kind=kOutput, calls=%fused_computation.2.clone.1 | convolution fusion | flops 52428800 | bytes 738308 | tf_op jit(solution)/shard_map/while/body/eval_jaxpr/dot_general | solution.py:28
  86.1 0.6 dynamic_slice.52
  88.7 2.0 %fusion.12 = bf16[16,128,320]{1,2,0:T(8,128)(2,1)} fusion(bf16[16,128,320]{1,2,0:T(8,128)(2,1)} %get-tuple-element.89, s32[]{:T(128)} %get-tuple-element.88, bf16[8,640,320]{1,2,0:T(8,128)(2,1)} %get-tuple-element.100, s32[]{:T(128)S(6)} %select_n.103, bf16[16,128,640]{2,1,0:T(8,128)(2,1)} %get-tuple-element.98), kind=kOutput, calls=%fused_computation.2.clone.1 | convolution fusion | flops 52428800 | bytes 738308 | tf_op jit(solution)/shard_map/while/body/eval_jaxpr/dot_general | solution.py:28
  90.7 0.6 dynamic_slice.52
  93.2 2.0 %fusion.12 = bf16[16,128,320]{1,2,0:T(8,128)(2,1)} fusion(bf16[16,128,320]{1,2,0:T(8,128)(2,1)} %get-tuple-element.89, s32[]{:T(128)} %get-tuple-element.88, bf16[8,640,320]{1,2,0:T(8,128)(2,1)} %get-tuple-element.100, s32[]{:T(128)S(6)} %select_n.103, bf16[16,128,640]{2,1,0:T(8,128)(2,1)} %get-tuple-element.98), kind=kOutput, calls=%fused_computation.2.clone.1 | convolution fusion | flops 52428800 | bytes 738308 | tf_op jit(solution)/shard_map/while/body/eval_jaxpr/dot_general | solution.py:28
  95.3 0.6 dynamic_slice.52
  97.8 2.0 %fusion.12 = bf16[16,128,320]{1,2,0:T(8,128)(2,1)} fusion(bf16[16,128,320]{1,2,0:T(8,128)(2,1)} %get-tuple-element.89, s32[]{:T(128)} %get-tuple-element.88, bf16[8,640,320]{1,2,0:T(8,128)(2,1)} %get-tuple-element.100, s32[]{:T(128)S(6)} %select_n.103, bf16[16,128,640]{2,1,0:T(8,128)(2,1)} %get-tuple-element.98), kind=kOutput, calls=%fused_computation.2.clone.1 | convolution fusion | flops 52428800 | bytes 738308 | tf_op jit(solution)/shard_map/while/body/eval_jaxpr/dot_general | solution.py:28
  99.8 0.6 dynamic_slice.52
  102.4 2.0 %fusion.12 = bf16[16,128,320]{1,2,0:T(8,128)(2,1)} fusion(bf16[16,128,320]{1,2,0:T(8,128)(2,1)} %get-tuple-element.89, s32[]{:T(128)} %get-tuple-element.88, bf16[8,640,320]{1,2,0:T(8,128)(2,1)} %get-tuple-element.100, s32[]{:T(128)S(6)} %select_n.103, bf16[16,128,640]{2,1,0:T(8,128)(2,1)} %get-tuple-element.98), kind=kOutput, calls=%fused_computation.2.clone.1 | convolution fusion | flops 52428800 | bytes 738308 | tf_op jit(solution)/shard_map/while/body/eval_jaxpr/dot_general | solution.py:28
  104.4 0.6 dynamic_slice.52
  106.9 2.0 %fusion.12 = bf16[16,128,320]{1,2,0:T(8,128)(2,1)} fusion(bf16[16,128,320]{1,2,0:T(8,128)(2,1)} %get-tuple-element.89, s32[]{:T(128)} %get-tuple-element.88, bf16[8,640,320]{1,2,0:T(8,128)(2,1)} %get-tuple-element.100, s32[]{:T(128)S(6)} %select_n.103, bf16[16,128,640]{2,1,0:T(8,128)(2,1)} %get-tuple-element.98), kind=kOutput, calls=%fused_computation.2.clone.1 | convolution fusion | flops 52428800 | bytes 738308 | tf_op jit(solution)/shard_map/while/body/eval_jaxpr/dot_general | solution.py:28
  108.9 2.2 %copy.5 = bf16[16,128,320]{1,0,2:T(8,128)(2,1)S(1)} copy(bf16[16,128,320]{1,2,0:T(8,128)(2,1)} %get-tuple-element.32) | data formatting | bytes 2621440
  111.1 1.4 copy.10
  112.5 0.0 reduce-scatter.4.cloned.1.call-update
  112.5 57.3 %reduce-scatter.4.cloned.1.call-done = bf16[40,2048]{1,0:T(8,128)(2,1)} async-done(((bf16[320,2048]{1,0:T(8,128)(2,1)}), bf16[40,2048]{1,0:T(8,128)(2,1)}) %reduce-scatter.4.cloned.1.call-update) | async-done | bytes 163856
  169.8 0.9 copy.8
  170.8 0.7 copy.6
  (4 shorter events, 0.0 us)
Async XLA Ops:
  6.5 9.5 %copy-start = (s32[8]{0:T(128)S(1)}, s32[8]{0:T(128)}, u32[]{:S(2)}) copy-start(s32[8]{0:T(128)} %param.8) | copy-start | bytes 100
  6.5 163.3 %reduce-scatter.4.cloned.1.call-start = ((), (), s32[]{:S(2)}) async-start(), calls=%async_computation.1 | async-start | bytes 1474560
  10.1 11.6 %collective-permute-start = (bf16[4,128,640]{2,1,0:T(8,128)(2,1)S(1)}, bf16[4,128,640]{2,1,0:T(8,128)(2,1)S(1)}, u32[]{:S(2)}, u32[]{:S(2)}) collective-permute-start(bf16[4,128,640]{2,1,0:T(8,128)(2,1)S(1)} %get-tuple-element.43), channel_id=1, source_target_pairs={{0,8},{8,16},{16,24},{24,32},{32,40},{40,48},{48,56},{56,64},{64,7... | collective-permute-start | bytes 1966088 | tf_op jit(solution)/shard_map/ppermute | solution.py:13
  14.2 11.3 %collective-permute-start.1 = (bf16[4,128,640]{2,1,0:T(8,128)(2,1)S(1)}, bf16[4,128,640]{2,1,0:T(8,128)(2,1)S(1)}, u32[]{:S(2)}, u32[]{:S(2)}) collective-permute-start(bf16[4,128,640]{2,1,0:T(8,128)(2,1)S(1)} %get-tuple-element.44), channel_id=1, source_target_pairs={{8,0},{16,8},{24,16},{32,24},{40,32},{48,40},{56,48},{64,56},{72,6... | collective-permute-start | bytes 1966088 | tf_op jit(solution)/shard_map/ppermute | solution.py:13
Sparse Core Ops, SparseCore 0:
  112.7 57.1 reduce-scatter.3
where the time goes:
time: 179 us; the launch traced here: 178 us
  waiting for transfers between devices  61.6 us (34%)
  matrix products  32 us (18%)
  loops' own time  30.5 us (17%)
  local copies, waits for them, and re-layouts  22 us (12%)
  between operations  14.7 us (8%)
  other arithmetic  12.2 us (7%)
  starting transfers between devices  5.37 us (3%)
    unnamed x2, waiting for transfers between devices  57.3 us
    dot_general x16, matrix products, one_block(): return jnp.dot(amplitude_tile, weights, preferred_element_type=jnp.float32)  32 us
    another operation x1, loops' own time, contract(): return lax.map(one_block, (amplitudes, sectors))  30.5 us
    dynamic_slice x16, local copies, waits for them, and re-layouts, contract(): return lax.map(one_block, (amplitudes, sectors))  10.4 us
    ppermute x2, starting transfers between devices, from_behind(): return lax.ppermute(block, axis, route)  5.36 us
    unnamed x6, local copies, waits for them, and re-layouts  5.23 us
    concatenate x1, other arithmetic, assemble(): joined = jnp.concatenate([from_left, blocks_held, from_right], axis=0)  5.13 us
    select_n x2, other arithmetic, assemble(): return jnp.take(joined, picked, axis=0)  4.3 us
  transfers between devices with their start and end apart: 3, of which 3 were waited for; matrix products, arithmetic and copies ran while one was open for 3% of the time, Pallas kernels for 0%

commit v1 on v0

v1 whole, which is shorter than its diff:
```python
import functools

import jax
import jax.numpy as jnp
from jax import lax
from jax.experimental import pallas as pl
from jax.experimental.pallas import tpu as pltpu
from jax.sharding import PartitionSpec as P

BLK_DEV = 16
SHIFT_MOST = 4
PARTS = 8
HALF = 4


def contract_kernel(groups, tiles_ref, offsets_ref, t2_ref, weights_ref, *rest):
    outs = rest[: len(groups)]
    tiles, weights, tile_sems, weight_sems = rest[len(groups):]
    device = lax.axis_index("blk")
    rep = lax.axis_index("rep")
    first = offsets_ref[0, device]
    last = offsets_ref[1, device] - 1
    sector_count, width, _ = weights_ref.shape
    ends = []
    total = jnp.int32(0)
    for s in range(sector_count):
        total = total + tiles_ref[s]
        ends.append(total)

    blocks, sectors = [], []
    for start, count in groups:
        for j in range(count):
            block = jnp.clip(device * BLK_DEV + (start + j), first, last)
            sector = jnp.int32(0)
            for s in range(sector_count - 1):
                sector = sector + (ends[s] <= block).astype(jnp.int32)
            blocks.append(block)
            sectors.append(sector)

    def weight_copy(s):
        return pltpu.make_async_copy(weights_ref.at[s], weights.at[s], weight_sems.at[s])

    def tile_copy(j):
        return pltpu.make_async_copy(t2_ref.at[blocks[j] - first], tiles.at[j], tile_sems.at[j])

    def at_new_sector(j, step):
        if j == 0:
            step()
        else:
            pl.when(sectors[j] != sectors[j - 1])(step)

    for j in range(len(blocks)):
        at_new_sector(j, lambda: weight_copy(sectors[j]).start())
        tile_copy(j).start()

    half = width // 2
    columns = width // PARTS
    at = 0
    for g, (start, count) in enumerate(groups):
        for pair in range(count // 2):
            for j in (at, at + 1):
                at_new_sector(j, lambda: weight_copy(sectors[j]).wait())
                tile_copy(j).wait()
            for side in range(2):
                of_rep = pl.ds(pl.multiple_of((rep ^ side) * half, half), half)
                products = [
                    lax.dot_general(
                        weights[sectors[j], of_rep, :], tiles[j], (((1,), (1,)), ((), ())),
                        preferred_element_type=jnp.float32,
                    )
                    for j in (at, at + 1)
                ]
                for part in range(HALF):
                    rows = slice(part * columns, (part + 1) * columns)
                    both = jnp.concatenate([value[rows] for value in products], axis=0)
                    at_rows = slice(pair * 2 * columns, (pair + 1) * 2 * columns)
                    outs[g][side * HALF + part, at_rows, :] = both.astype(outs[g].dtype)
            at += 2


def contract(groups, sector_tiles, offsets, t2, weights):
    used = sum(count for _, count in groups)
    sectors, width, depth = weights.shape
    rows = t2.shape[1]
    shapes = [
        jax.ShapeDtypeStruct((PARTS, count * (width // PARTS), rows), jnp.bfloat16)
        for _, count in groups
    ]
    return pl.pallas_call(
        functools.partial(contract_kernel, groups),
        out_shape=shapes,
        in_specs=[
            pl.BlockSpec(memory_space=pltpu.SMEM),
            pl.BlockSpec(memory_space=pltpu.SMEM),
            pl.BlockSpec(memory_space=pltpu.HBM),
            pl.BlockSpec(memory_space=pltpu.HBM),
        ],
        out_specs=[pl.BlockSpec(memory_space=pltpu.VMEM)] * len(shapes),
        scratch_shapes=[
            pltpu.VMEM((used, rows, depth), t2.dtype),
            pltpu.VMEM((sectors, width, depth), weights.dtype),
            pltpu.SemaphoreType.DMA((used,)),
            pltpu.SemaphoreType.DMA((sectors,)),
        ],
        cost_estimate=pl.CostEstimate(
            flops=2 * used * rows * depth * width,
            bytes_accessed=2 * (used * rows * depth + used * rows * width),
            transcendentals=0,
        ),
        compiler_params=pltpu.CompilerParams(vmem_limit_bytes=52 * 1024 * 1024),
    )(sector_tiles, offsets, t2, weights)


def merge_kernel(offsets_ref, own, left, right, kept, given):
    device = lax.axis_index("blk")
    first = offsets_ref[0, device]
    end = offsets_ref[1, device]
    size, edge = own.shape[1], left.shape[1]
    columns = edge // SHIFT_MOST
    base = device * BLK_DEV
    row = lax.broadcasted_iota(jnp.int32, (edge, own.shape[2]), 0)
    below = row < (first - base) * columns
    above = row >= (end - (base + BLK_DEV - SHIFT_MOST)) * columns
    middle = slice(edge, size - edge)
    for part in range(PARTS):
        out = (kept, given)[part // HALF]
        at = part % HALF
        for mask, other, rows in (
            (below, left, slice(0, edge)),
            (above, right, slice(size - edge, size)),
        ):
            value = jnp.where(
                mask, other[part].astype(jnp.float32), own[part, rows, :].astype(jnp.float32)
            )
            out[at, rows, :] = value.astype(out.dtype)
        out[at, middle, :] = own[part, middle, :]


def merge(offsets, own, left, right):
    vmem = pl.BlockSpec(memory_space=pltpu.VMEM)
    half = jax.ShapeDtypeStruct((HALF,) + own.shape[1:], own.dtype)
    return pl.pallas_call(
        merge_kernel,
        out_shape=[half] * 2,
        in_specs=[pl.BlockSpec(memory_space=pltpu.SMEM)] + [vmem] * 3,
        out_specs=[vmem] * 2,
        cost_estimate=pl.CostEstimate(flops=0, bytes_accessed=4 * own.size, transcendentals=0),
        compiler_params=pltpu.CompilerParams(vmem_limit_bytes=8 * 1024 * 1024),
    )(offsets, own, left, right)


def shifted(block, axis, distance):
    count = lax.axis_size(axis)
    route = [(i, i + distance) for i in range(count) if 0 <= i + distance < count]
    return lax.ppermute(block, axis, route)


def per_device(t2_source, integrals, sector_tiles, block_offsets):
    offsets = jnp.swapaxes(block_offsets, 0, 1)
    weights = jnp.swapaxes(integrals, 1, 2)

    leftward, rightward = contract(
        ((-SHIFT_MOST, SHIFT_MOST), (BLK_DEV, SHIFT_MOST)), sector_tiles, offsets, t2_source, weights
    )
    from_left = shifted(rightward, "blk", 1)
    from_right = shifted(leftward, "blk", -1)
    (own,) = contract(((0, BLK_DEV),), sector_tiles, offsets, t2_source, weights)

    kept, given = merge(offsets, own, from_left, from_right)
    taken = lax.ppermute(given, "rep", [(0, 1), (1, 0)])
    chip = (kept.astype(jnp.float32) + taken.astype(jnp.float32)).astype(jnp.bfloat16)
    chunks = lax.all_to_all(chip, "slab", 0, 0, tiled=True)
    a, b, c, d = (chunks[i].astype(jnp.float32) for i in range(HALF))
    total = ((a + b) + (c + d)).astype(jnp.bfloat16)
    return jnp.swapaxes(total.reshape(BLK_DEV, -1, total.shape[1]), 1, 2)


def solution(mesh):
    in_specs = (P("blk", None, ("rep", "slab")), P(None, ("rep", "slab"), None), P(), P())
    out_specs = P("blk", None, ("rep", "slab"))
    return jax.shard_map(
        per_device, mesh=mesh, in_specs=in_specs, out_specs=out_specs, check_vma=False
    )
```

time: 179 us -> 45.1 us (0.25)
  the two profiles are of different devices: /device:TPU:1 before, /device:TPU:248 now
where the time goes in v1:
time: 45.1 us; the launch traced here: 44.9 us
  blocking collectives  15.3 us (34%)
  Pallas kernels  9.4 us (21%)
  waiting for transfers between devices  9.32 us (21%)
  starting transfers between devices  8.54 us (19%)
  local copies, waits for them, and re-layouts  1.33 us (3%)
  other arithmetic  0.93 us (2%)
    all_to_all x1, blocking collectives, per_device(): chunks = lax.all_to_all(chip, 'slab', 0, 0, tiled=True)  15.3 us
    pallas_call x2, Pallas kernels, contract(): pl.pallas_call(functools.partial(contract_kernel, groups), out_shape=shap...  8.63 us
    ppermute x2, waiting for transfers between devices, shifted(): return lax.ppermute(block, axis, route)  7.26 us
    ppermute x2, starting transfers between devices, shifted(): return lax.ppermute(block, axis, route)  6.62 us
    ppermute x1, waiting for transfers between devices, per_device(): taken = lax.ppermute(given, 'rep', [(0, 1), (1, 0)])  2.06 us
    ppermute x1, starting transfers between devices, per_device(): taken = lax.ppermute(given, 'rep', [(0, 1), (1, 0)])  1.92 us
    unnamed x4, local copies, waits for them, and re-layouts  1.33 us
  transfers between devices with their start and end apart: 3, of which 2 were waited for; matrix products, arithmetic and copies ran while one was open for 0% of the time, Pallas kernels for 12%

profile of v1, /device:TPU:248, one launch (start us, length us, event | category | flops | bytes accessed | tf_op | source)
XLA Modules:
  0.0 44.9 jit_solution(12642401561594595776)
XLA Ops:
  0.0 0.0 copy-start
  0.0 0.7 %copy-done = s32[96,2]{0,1:T(2,128)S(1)} copy-done((s32[96,2]{0,1:T(2,128)S(1)}, s32[96,2]{0,1:T(2,128)}, u32[]{:S(2)}) %copy-start) | copy-done | bytes 792
  0.7 0.0 copy-start.1
  0.7 0.7 %copy-done.1 = s32[8]{0:T(128)S(1)} copy-done((s32[8]{0:T(128)S(1)}, s32[8]{0:T(128)}, u32[]{:S(2)}) %copy-start.1) | copy-done | bytes 56
  1.3 3.4 %shard_map.47 = (bf16[8,160,128]{2,1,0:T(8,128)(2,1)S(1)}, bf16[8,160,128]{2,1,0:T(8,128)(2,1)S(1)}) custom-call(s32[8]{0:T(128)S(1)} %copy-done.1, s32[2,96]{1,0:T(2,128)S(1)} %bitcast.5, bf16[24,128,640]{2,1,0:T(8,128)(2,1)} %t2_ref.3, bf16[8,320,640]{2,1,0:T(8,128)(2,1)} %bitcast.8), custom_call_target="tpu_custom_call" | custom-call | flops 419430400 | bytes 1966080 | tf_op jit(solution)/shard_map/pallas_call | solution.py:89
  4.8 4.7 %collective-permute-start = (bf16[8,160,128]{2,1,0:T(8,128)(2,1)S(1)}, bf16[8,160,128]{2,1,0:T(8,128)(2,1)S(1)}, u32[]{:S(2)}, u32[]{:S(2)}) collective-permute-start(bf16[8,160,128]{2,1,0:T(8,128)(2,1)S(1)} %get-tuple-element.9), channel_id=1, source_target_pairs={{0,8},{8,16},{16,24},{24,32},{32,40},{40,48},{48,56},{56,64},{64,7... | collective-permute-start | bytes 983048 | tf_op jit(solution)/shard_map/ppermute | solution.py:155
  9.5 1.9 %collective-permute-start.1 = (bf16[8,160,128]{2,1,0:T(8,128)(2,1)S(1)}, bf16[8,160,128]{2,1,0:T(8,128)(2,1)S(1)}, u32[]{:S(2)}, u32[]{:S(2)}) collective-permute-start(bf16[8,160,128]{2,1,0:T(8,128)(2,1)S(1)} %get-tuple-element.10), channel_id=1, source_target_pairs={{8,0},{16,8},{24,16},{32,24},{40,32},{48,40},{56,48},{64,56},{72,6... | collective-permute-start | bytes 983048 | tf_op jit(solution)/shard_map/ppermute | solution.py:155
  11.4 5.2 %shard_map.46.own = bf16[8,640,128]{2,1,0:T(8,128)(2,1)S(1)} custom-call(s32[8]{0:T(128)S(1)} %copy-done.1, s32[2,96]{1,0:T(2,128)S(1)} %bitcast.6, bf16[24,128,640]{2,1,0:T(8,128)(2,1)} %t2_ref.3, bf16[8,320,640]{2,1,0:T(8,128)(2,1)} %bitcast.9), custom_call_target="tpu_custom_call" | custom-call | flops 838860800 | bytes 3932160 | tf_op jit(solution)/shard_map/pallas_call | solution.py:89
  16.6 0.0 collective-permute-done.left
  16.6 7.3 %collective-permute-done.1.right = bf16[8,160,128]{2,1,0:T(8,128)(2,1)S(1)} collective-permute-done((bf16[8,160,128]{2,1,0:T(8,128)(2,1)S(1)}, bf16[8,160,128]{2,1,0:T(8,128)(2,1)S(1)}, u32[]{:S(2)}, u32[]{:S(2)}) %collective-permute-start.1) | collective-permute-done | bytes 327712 | tf_op jit(solution)/shard_map/ppermute | solution.py:155
  23.9 0.8 %shard_map.48 = (bf16[4,640,128]{2,1,0:T(8,128)(2,1)S(1)}, bf16[4,640,128]{2,1,0:T(8,128)(2,1)S(1)}) custom-call(s32[2,96]{1,0:T(2,128)S(1)} %bitcast.7, bf16[8,640,128]{2,1,0:T(8,128)(2,1)S(1)} %shard_map.46.own, bf16[8,160,128]{2,1,0:T(8,128)(2,1)S(1)} %collective-permute-done.left, bf16[8,160,128]{2,1,0:T(8,128)(2,1)S(1)} %collective-permute-done.1.right), custom_call_target="tpu_custom_call" | custom-call | bytes 2621440 | tf_op jit(solution)/shard_map/pallas_call | solution.py:142
  24.7 1.9 %collective-permute-start.2 = (bf16[4,640,128]{2,1,0:T(8,128)(2,1)S(1)}, bf16[4,640,128]{2,1,0:T(8,128)(2,1)S(1)}, u32[]{:S(2)}, u32[]{:S(2)}) collective-permute-start(bf16[4,640,128]{2,1,0:T(8,128)(2,1)S(1)} %get-tuple-element.12), channel_id=1, source_target_pairs={{0,4},{4,0},{1,5},{5,1},{2,6},{6,2},{3,7},{7,3},{8,12},{12,8},{9,1... | collective-permute-start | bytes 1966088 | tf_op jit(solution)/shard_map/ppermute | solution.py:170
  26.6 2.1 %collective-permute-done.2 = bf16[4,640,128]{2,1,0:T(8,128)(2,1)S(1)} collective-permute-done((bf16[4,640,128]{2,1,0:T(8,128)(2,1)S(1)}, bf16[4,640,128]{2,1,0:T(8,128)(2,1)S(1)}, u32[]{:S(2)}, u32[]{:S(2)}) %collective-permute-start.2) | collective-permute-done | bytes 655392 | tf_op jit(solution)/shard_map/ppermute | solution.py:170
  28.7 0.2 add_convert_fusion
  28.8 15.3 %all_to_all.5 = bf16[4,640,128]{2,1,0:T(8,128)(2,1)S(1)} all-to-all(bf16[4,640,128]{2,1,0:T(8,128)(2,1)S(1)} %add_convert_fusion), channel_id=1, replica_groups=mesh['blk'=96,'rep'=2,'slab'=4] {'slab'}, dimensions={0} | all-to-all | bytes 1310720 | tf_op jit(solution)/shard_map/all_to_all | solution.py:172
  44.1 0.8 %add_convert_fusion.1 = bf16[1,640,128]{2,1,0:T(8,128)(2,1)} fusion(bf16[4,640,128]{2,1,0:T(8,128)(2,1)S(1)} %all_to_all.5), kind=kLoop, calls=%fused_computation.1 | loop fusion | flops 655360 | bytes 819200 | tf_op jit(solution)/shard_map/convert_element_type | solution.py:174
Async XLA Ops:
  0.0 0.7 %copy-start = (s32[96,2]{0,1:T(2,128)S(1)}, s32[96,2]{0,1:T(2,128)}, u32[]{:S(2)}) copy-start(s32[96,2]{0,1:T(2,128)} %param.7) | copy-start | bytes 2308
  0.7 0.7 %copy-start.1 = (s32[8]{0:T(128)S(1)}, s32[8]{0:T(128)}, u32[]{:S(2)}) copy-start(s32[8]{0:T(128)} %tiles_ref.3) | copy-start | bytes 100
  4.8 11.8 %collective-permute-start = (bf16[8,160,128]{2,1,0:T(8,128)(2,1)S(1)}, bf16[8,160,128]{2,1,0:T(8,128)(2,1)S(1)}, u32[]{:S(2)}, u32[]{:S(2)}) collective-permute-start(bf16[8,160,128]{2,1,0:T(8,128)(2,1)S(1)} %get-tuple-element.9), channel_id=1, source_target_pairs={{0,8},{8,16},{16,24},{24,32},{32,40},{40,48},{48,56},{56,64},{64,7... | collective-permute-start | bytes 983048 | tf_op jit(solution)/shard_map/ppermute | solution.py:155
  9.5 14.4 %collective-permute-start.1 = (bf16[8,160,128]{2,1,0:T(8,128)(2,1)S(1)}, bf16[8,160,128]{2,1,0:T(8,128)(2,1)S(1)}, u32[]{:S(2)}, u32[]{:S(2)}) collective-permute-start(bf16[8,160,128]{2,1,0:T(8,128)(2,1)S(1)} %get-tuple-element.10), channel_id=1, source_target_pairs={{8,0},{16,8},{24,16},{32,24},{40,32},{48,40},{56,48},{64,56},{72,6... | collective-permute-start | bytes 983048 | tf_op jit(solution)/shard_map/ppermute | solution.py:155
  24.7 4.0 %collective-permute-start.2 = (bf16[4,640,128]{2,1,0:T(8,128)(2,1)S(1)}, bf16[4,640,128]{2,1,0:T(8,128)(2,1)S(1)}, u32[]{:S(2)}, u32[]{:S(2)}) collective-permute-start(bf16[4,640,128]{2,1,0:T(8,128)(2,1)S(1)} %get-tuple-element.12), channel_id=1, source_target_pairs={{0,4},{4,0},{1,5},{5,1},{2,6},{6,2},{3,7},{7,3},{8,12},{12,8},{9,1... | collective-permute-start | bytes 1966088 | tf_op jit(solution)/shard_map/ppermute | solution.py:170

commit v2 on v0

v2 whole, which is shorter than its diff:
```python
import jax
import jax.numpy as jnp
from jax import lax
from jax.experimental import pallas as pl
from jax.experimental.pallas import tpu as pltpu
from jax.sharding import PartitionSpec as P

BLK_DEV = 16
SHIFT_MOST = 4
PARTS = 8
HALF = 4
MIB = 1024 * 1024


def product_pairs(weights, sectors, tiles, store):
    def dot(sector, tile):
        return lax.dot_general(
            weights[sector], tile, (((1,), (1,)), ((), ())), preferred_element_type=jnp.float32
        )

    pairs = len(tiles) // 2
    for pair in range(pairs):
        left, right = tiles[2 * pair][...], tiles[2 * pair + 1][...]
        both = dot(sectors[2 * pair], jnp.concatenate([left, right], axis=0))
        store(pair, both[:, : left.shape[0]], both[:, left.shape[0] :])

    for pair in range(pairs):
        left, right = sectors[2 * pair], sectors[2 * pair + 1]

        @pl.when(left != right)
        def _():
            store(pair, dot(left, tiles[2 * pair][...]), dot(right, tiles[2 * pair + 1][...]))


def interleaved(a, b, columns, outs, at):
    for part, out in enumerate(outs):
        rows = slice(part * columns, (part + 1) * columns)
        both = jnp.concatenate([a[rows], b[rows]], axis=0)
        out[at : at + 2 * columns, :] = both.astype(out.dtype)


def outward_kernel(
    sector_tiles, block_offsets, t2, integrals, kept, given, tiles, weights, info,
    counts, offsets, upper, count_sem, offset_sem, tile_sems, weight_sems,
):
    device = lax.axis_index("blk")
    rep = lax.axis_index("rep")
    sector_count, width, _ = integrals.shape
    reach = tiles.shape[0]
    half = width // 2
    columns = width // PARTS

    small = [
        pltpu.make_async_copy(block_offsets, offsets, offset_sem),
        pltpu.make_async_copy(sector_tiles, counts, count_sem),
    ]
    lower = pltpu.make_async_copy(
        t2.at[pl.ds(0, SHIFT_MOST)], tiles.at[pl.ds(0, SHIFT_MOST)], tile_sems.at[0]
    )
    for copy in small + [lower]:
        copy.start()
    for copy in small:
        copy.wait()

    first = offsets[0, device]
    last = offsets[1, device] - 1
    ends = []
    total = jnp.int32(0)
    for s in range(sector_count):
        total = total + counts[s]
        ends.append(total)

    def each_weight(step):
        for s in range(sector_count):
            begin = ends[s - 1] if s else jnp.int32(0)

            @pl.when((begin <= last) & (first < ends[s]))
            def _():
                for side in range(2):
                    from_row = pl.multiple_of((rep ^ side) * half, half)
                    step(
                        pltpu.make_async_copy(
                            integrals.at[s, pl.ds(from_row, half)],
                            weights.at[s, pl.ds(side * half, half)],
                            weight_sems.at[s, side],
                        )
                    )

    base = device * BLK_DEV
    each_weight(lambda copy: copy.start())
    above = pltpu.make_async_copy(
        t2.at[pl.ds(jnp.clip(base + BLK_DEV - first, 0, t2.shape[0] - SHIFT_MOST), SHIFT_MOST)],
        upper,
        tile_sems.at[1],
    )
    others = pltpu.make_async_copy(
        t2.at[pl.ds(SHIFT_MOST, reach - SHIFT_MOST)],
        tiles.at[pl.ds(SHIFT_MOST, reach - SHIFT_MOST)],
        tile_sems.at[2],
    )
    above.start()
    others.start()

    def sector_of(block):
        held = jnp.clip(block, first, last)
        sector = jnp.int32(0)
        for s in range(sector_count - 1):
            sector = sector + (ends[s] <= held).astype(jnp.int32)
        return sector

    outside = list(range(-SHIFT_MOST, 0)) + list(range(BLK_DEV, BLK_DEV + SHIFT_MOST))
    sectors = [sector_of(base + j) for j in outside]
    edges = [
        tiles.at[jnp.clip(base - SHIFT_MOST + j - first, 0, SHIFT_MOST - 1)]
        for j in range(SHIFT_MOST)
    ] + [upper.at[j] for j in range(SHIFT_MOST)]

    for j in range(BLK_DEV):
        info[j] = sector_of(base + j)
        info[BLK_DEV + j] = jnp.clip(base + j - first, 0, reach - 1)
    info[2 * BLK_DEV] = first - base
    info[2 * BLK_DEV + 1] = last + 1 - base
    info[2 * BLK_DEV + 2] = rep

    def store(pair, a, b):
        group, at = divmod(pair, SHIFT_MOST // 2)
        outs = [out.at[group, part] for out in (kept, given) for part in range(HALF)]
        interleaved(a, b, columns, outs, at * 2 * columns)

    lower.wait()
    each_weight(lambda copy: copy.wait())
    above.wait()
    product_pairs(weights, sectors, edges, store)
    others.wait()


def outward(sector_tiles, offsets, t2, integrals):
    sectors, width, depth = integrals.shape
    rows = t2.shape[1]
    out = jax.ShapeDtypeStruct((2, HALF, SHIFT_MOST * (width // PARTS), rows), jnp.bfloat16)
    hbm = pl.BlockSpec(memory_space=pltpu.HBM)
    vmem = pl.BlockSpec(memory_space=pltpu.VMEM)
    args = [
        pltpu.with_memory_space_constraint(x, pltpu.HBM)
        for x in (sector_tiles, offsets, t2, integrals)
    ]
    return pl.pallas_call(
        outward_kernel,
        out_shape=[
            out,
            out,
            jax.ShapeDtypeStruct((BLK_DEV + SHIFT_MOST, rows, depth), t2.dtype),
            jax.ShapeDtypeStruct(integrals.shape, integrals.dtype),
            pltpu.SMEM((128,), jnp.int32),
        ],
        in_specs=[hbm] * 4,
        out_specs=[vmem] * 4 + [pl.BlockSpec(memory_space=pltpu.SMEM)],
        scratch_shapes=[
            pltpu.SMEM(sector_tiles.shape, jnp.int32),
            pltpu.SMEM(offsets.shape, jnp.int32),
            pltpu.VMEM((SHIFT_MOST, rows, depth), t2.dtype),
            pltpu.SemaphoreType.DMA(()),
            pltpu.SemaphoreType.DMA(()),
            pltpu.SemaphoreType.DMA((3,)),
            pltpu.SemaphoreType.DMA((sectors, 2)),
        ],
        cost_estimate=pl.CostEstimate(
            flops=4 * SHIFT_MOST * rows * depth * width,
            bytes_accessed=2 * t2.size,
            transcendentals=0,
        ),
        compiler_params=pltpu.CompilerParams(vmem_limit_bytes=24 * MIB),
    )(*args)


def own_kernel(info, tiles, weights, partial):
    columns = weights.shape[1] // PARTS
    rep = info[2 * BLK_DEV + 2]

    def store(pair, a, b):
        outs = [partial.at[rep ^ side, part] for side in range(2) for part in range(HALF)]
        interleaved(a, b, columns, outs, pair * 2 * columns)

    sectors = [info[j] for j in range(BLK_DEV)]
    slots = [tiles.at[info[BLK_DEV + j]] for j in range(BLK_DEV)]
    product_pairs(weights, sectors, slots, store)


def own(info, tiles, weights):
    _, width, depth = weights.shape
    rows = tiles.shape[1]
    vmem = pl.BlockSpec(memory_space=pltpu.VMEM)
    return pl.pallas_call(
        own_kernel,
        out_shape=jax.ShapeDtypeStruct(
            (2, HALF, BLK_DEV * (width // PARTS), rows), jnp.bfloat16
        ),
        in_specs=[pl.BlockSpec(memory_space=pltpu.SMEM)] + [vmem] * 2,
        out_specs=vmem,
        cost_estimate=pl.CostEstimate(
            flops=2 * BLK_DEV * rows * depth * width,
            bytes_accessed=2 * (tiles.size + BLK_DEV * rows * width),
            transcendentals=0,
        ),
        compiler_params=pltpu.CompilerParams(vmem_limit_bytes=24 * MIB),
    )(pltpu.with_memory_space_constraint(info, pltpu.SMEM), tiles, weights)


def combine_kernel(info, pieces, left, right, chip):
    size, edge = chip.shape[1], left.shape[1]
    columns = edge // SHIFT_MOST
    row = lax.broadcasted_iota(jnp.int32, (edge, chip.shape[2]), 0)
    below = row < info[2 * BLK_DEV] * columns
    above = row >= (info[2 * BLK_DEV + 1] - (BLK_DEV - SHIFT_MOST)) * columns
    for part in range(HALF):
        for mask, other, rows in (
            (below, left, slice(0, edge)),
            (None, None, slice(edge, size - edge)),
            (above, right, slice(size - edge, size)),
        ):
            value = pieces[0, part, rows, :].astype(jnp.float32)
            value = value + pieces[1, part, rows, :].astype(jnp.float32)
            if mask is not None:
                value = jnp.where(mask, other[part].astype(jnp.float32), value)
            chip[part, rows, :] = value.astype(chip.dtype)


def combine(info, pieces, left, right):
    vmem = pl.BlockSpec(memory_space=pltpu.VMEM)
    return pl.pallas_call(
        combine_kernel,
        out_shape=jax.ShapeDtypeStruct(pieces.shape[1:], pieces.dtype),
        in_specs=[pl.BlockSpec(memory_space=pltpu.SMEM)] + [vmem] * 3,
        out_specs=vmem,
        cost_estimate=pl.CostEstimate(
            flops=pieces.size, bytes_accessed=4 * pieces.size, transcendentals=0
        ),
        compiler_params=pltpu.CompilerParams(vmem_limit_bytes=8 * MIB),
    )(pltpu.with_memory_space_constraint(info, pltpu.SMEM), pieces, left, right)


def shifted(block, axis, distance):
    count = lax.axis_size(axis)
    route = [(i, i + distance) for i in range(count) if 0 <= i + distance < count]
    return lax.ppermute(block, axis, route)


def swapped(block):
    return lax.ppermute(block, "rep", [(0, 1), (1, 0)])


def per_device(t2_source, integrals, sector_tiles, block_offsets):
    offsets = jnp.swapaxes(block_offsets, 0, 1)
    weights = jnp.swapaxes(integrals, 1, 2)

    kept_out, given_out, tiles, weights, info = outward(sector_tiles, offsets, t2_source, weights)
    taken_out = swapped(given_out)
    partial = own(info, tiles, weights)
    leftward, rightward = (
        (kept_out[i].astype(jnp.float32) + taken_out[i].astype(jnp.float32)).astype(jnp.bfloat16)
        for i in range(2)
    )
    leftward, rightward, partial = lax.optimization_barrier((leftward, rightward, partial))
    from_left = shifted(rightward, "blk", 1)
    from_right = shifted(leftward, "blk", -1)

    pieces = lax.all_to_all(partial, "rep", 0, 0, tiled=True)
    chip = combine(info, pieces, from_left, from_right)
    chunks = lax.all_to_all(chip, "slab", 0, 0, tiled=True)
    a, b, c, d = (chunks[i].astype(jnp.float32) for i in range(HALF))
    total = ((a + b) + (c + d)).astype(jnp.bfloat16)
    return jnp.swapaxes(total.reshape(BLK_DEV, -1, total.shape[1]), 1, 2)


def solution(mesh):
    in_specs = (P("blk", None, ("rep", "slab")), P(None, ("rep", "slab"), None), P(), P())
    out_specs = P("blk", None, ("rep", "slab"))
    return jax.shard_map(
        per_device, mesh=mesh, in_specs=in_specs, out_specs=out_specs, check_vma=False
    )
```

time: 179 us -> 39.3 us (0.22)
  waiting for transfers between devices: 61.6 us -> 1.42 us
  matrix products: 32 us -> 0 us
  loops' own time: 30.5 us -> 0 us
  local copies, waits for them, and re-layouts: 22 us -> 0 us
  blocking collectives: 0 us -> 16.9 us
  between operations: 14.7 us -> 0.06 us
  other arithmetic: 12.2 us -> 0.84 us
  starting transfers between devices: 5.37 us -> 15 us
  Pallas kernels: 0 us -> 4.57 us
    unnamed x2 -> x0, waiting for transfers between devices: 57.3 us -> none
    dot_general x16 -> x0, matrix products: 32 us -> none  [one_block(): return jnp.dot(amplitude_tile, weights, preferred_element_type=jnp.float32)]
    another operation x1 -> x0, loops' own time: 30.5 us -> none  [contract(): return lax.map(one_block, (amplitudes, sectors))]
    all_to_all x0 -> x2, blocking collectives: none -> 16.9 us  [the longest x1 12.2 us: per_device(): chunks = lax.all_to_all(chip, 'slab', 0, 0, tiled=True)]
    dynamic_slice x18 -> x0, local copies, waits for them, and re-layouts: 13.3 us -> none  [the longest x16 10.4 us: contract(): return lax.map(one_block, (amplitudes, sectors))]
    ppermute x2 -> x3, starting transfers between devices: 5.36 us -> 15 us  [the longest x1 12.4 us: swapped(): return lax.ppermute(block, 'rep', [(0, 1), (1, 0)])]
    unnamed x6 -> x0, local copies, waits for them, and re-layouts: 5.23 us -> none
    concatenate x1 -> x0, other arithmetic: 5.13 us -> none  [assemble(): joined = jnp.concatenate([from_left, blocks_held, from_right], axis=0)]
  transfers between devices with their start and end apart: 3 -> 3, of which waited for: 3 -> 1; matrix products, arithmetic and copies ran while one was open for 3% -> 0% of each run, Pallas kernels for 0% -> 3%
where the time goes in v2:
time: 39.3 us; the launch traced here: 38.8 us
  blocking collectives  16.9 us (43%)
  starting transfers between devices  15 us (38%)
  Pallas kernels  4.57 us (12%)
  waiting for transfers between devices  1.42 us (4%)
  other arithmetic  0.84 us (2%)
    ppermute x1, starting transfers between devices, swapped(): return lax.ppermute(block, 'rep', [(0, 1), (1, 0)])  12.4 us
    all_to_all x1, blocking collectives, per_device(): chunks = lax.all_to_all(chip, 'slab', 0, 0, tiled=True)  12.2 us
    all_to_all x1, blocking collectives, per_device(): pieces = lax.all_to_all(partial, 'rep', 0, 0, tiled=True)  4.69 us
    pallas_call x1, Pallas kernels, outward(): pl.pallas_call(outward_kernel, out_shape=[out, out, jax.ShapeDtypeStruct(...  3.05 us
    ppermute x2, starting transfers between devices, shifted(): return lax.ppermute(block, axis, route)  2.59 us
    ppermute x2, waiting for transfers between devices, shifted(): return lax.ppermute(block, axis, route)  1.42 us
    pallas_call x1, Pallas kernels, own(): pl.pallas_call(own_kernel, out_shape=jax.ShapeDtypeStruct((2, HALF, BLK_D...  1.3 us
  transfers between devices with their start and end apart: 3, of which 1 were waited for; matrix products, arithmetic and copies ran while one was open for 0% of the time, Pallas kernels for 3%

profile of v2, /device:TPU:1, one launch (start us, length us, event | category | flops | bytes accessed | tf_op | source)
XLA Modules:
  0.0 38.8 jit_solution(16031190073125918155)
XLA Ops:
  0.0 3.0 %shard_map.46 = (bf16[2,4,160,128]{3,2,1,0:T(8,128)(2,1)S(1)}, bf16[2,4,160,128]{3,2,1,0:T(8,128)(2,1)S(1)}, bf16[20,128,640]{2,1,0:T(8,128)(2,1)S(1)}, bf16[8,320,640]{2,1,0:T(8,128)(2,1)S(1)}, s32[128]{0:T(128)S(4)}) custom-call(s32[8]{0:T(128)} %sector_tiles.1, s32[2,96]{1,0:T(2,128)} %bitcast.10, bf16[24,128,640]{2,1,0:T(8,128)(2,1)} %t2.1, ...), custom_call_target="tpu_custom_call" | custom-call | flops 419430400 | bytes 3932160 | tf_op jit(solution)/shard_map/pallas_call | solution.py:147
  3.1 12.4 %collective-permute-start = (bf16[2,4,160,128]{3,2,1,0:T(8,128)(2,1)S(1)}, bf16[2,4,160,128]{3,2,1,0:T(8,128)(2,1)S(1)}, u32[]{:S(2)}, u32[]{:S(2)}) collective-permute-start(bf16[2,4,160,128]{3,2,1,0:T(8,128)(2,1)S(1)} %get-tuple-element.15), channel_id=1, source_target_pairs={{0,4},{4,0},{1,5},{5,1},{2,6},{6,2},{3,7},{7,3},{8,12},{12,8},{9,1... | collective-permute-start | bytes 983048 | tf_op jit(solution)/shard_map/ppermute | solution.py:249
  15.5 1.3 %shard_map.47 = bf16[2,4,640,128]{3,2,1,0:T(8,128)(2,1)S(1)} custom-call(s32[128]{0:T(128)S(4)} %get-tuple-element.13.info, bf16[20,128,640]{2,1,0:T(8,128)(2,1)S(1)} %get-tuple-element.16.tiles, bf16[8,320,640]{2,1,0:T(8,128)(2,1)S(1)} %get-tuple-element.17.weights), custom_call_target="tpu_custom_call" | custom-call | flops 838860800 | bytes 4587520 | tf_op jit(solution)/shard_map/pallas_call | solution.py:193
  16.8 0.0 collective-permute-done
  16.8 0.1 fusion.1
  16.9 1.3 %collective-permute-start.1 = (bf16[4,160,128]{2,1,0:T(8,128)(2,1)S(1)}, bf16[4,160,128]{2,1,0:T(8,128)(2,1)S(1)}, u32[]{:S(2)}, u32[]{:S(2)}) collective-permute-start(bf16[4,160,128]{2,1,0:T(8,128)(2,1)S(1)} %get-tuple-element.19), channel_id=1, source_target_pairs={{0,8},{8,16},{16,24},{24,32},{32,40},{40,48},{48,56},{56,64},{64,7... | collective-permute-start | bytes 491528 | tf_op jit(solution)/shard_map/ppermute | solution.py:245
  18.2 1.3 %collective-permute-start.2 = (bf16[4,160,128]{2,1,0:T(8,128)(2,1)S(1)}, bf16[4,160,128]{2,1,0:T(8,128)(2,1)S(1)}, u32[]{:S(2)}, u32[]{:S(2)}) collective-permute-start(bf16[4,160,128]{2,1,0:T(8,128)(2,1)S(1)} %get-tuple-element.20), channel_id=1, source_target_pairs={{8,0},{16,8},{24,16},{32,24},{40,32},{48,40},{56,48},{64,56},{72,6... | collective-permute-start | bytes 491528 | tf_op jit(solution)/shard_map/ppermute | solution.py:245
  19.5 4.7 %all_to_all.10.pieces = bf16[2,4,640,128]{3,2,1,0:T(8,128)(2,1)S(1)} all-to-all(bf16[2,4,640,128]{3,2,1,0:T(8,128)(2,1)S(1)} %shard_map.47), channel_id=1, replica_groups=mesh['blk'=96,'rep'=2,'slab'=4] {'rep'}, dimensions={0} | all-to-all | bytes 2621440 | tf_op jit(solution)/shard_map/all_to_all | solution.py:267
  24.2 0.0 collective-permute-done.1.left
  24.2 1.4 %collective-permute-done.2.right = bf16[4,160,128]{2,1,0:T(8,128)(2,1)S(1)} collective-permute-done((bf16[4,160,128]{2,1,0:T(8,128)(2,1)S(1)}, bf16[4,160,128]{2,1,0:T(8,128)(2,1)S(1)}, u32[]{:S(2)}, u32[]{:S(2)}) %collective-permute-start.2) | collective-permute-done | bytes 163872 | tf_op jit(solution)/shard_map/ppermute | solution.py:245
  25.6 0.2 shard_map.48
  25.8 12.2 %all_to_all.11 = bf16[4,640,128]{2,1,0:T(8,128)(2,1)S(1)} all-to-all(bf16[4,640,128]{2,1,0:T(8,128)(2,1)S(1)} %shard_map.48), channel_id=1, replica_groups=mesh['blk'=96,'rep'=2,'slab'=4] {'slab'}, dimensions={0} | all-to-all | bytes 1310720 | tf_op jit(solution)/shard_map/all_to_all | solution.py:269
  38.1 0.8 %add_convert_fusion = bf16[1,640,128]{2,1,0:T(8,128)(2,1)} fusion(bf16[4,640,128]{2,1,0:T(8,128)(2,1)S(1)} %all_to_all.11), kind=kLoop, calls=%fused_computation | loop fusion | flops 655360 | bytes 819200 | tf_op jit(solution)/shard_map/convert_element_type | solution.py:271
Async XLA Ops:
  3.1 13.7 %collective-permute-start = (bf16[2,4,160,128]{3,2,1,0:T(8,128)(2,1)S(1)}, bf16[2,4,160,128]{3,2,1,0:T(8,128)(2,1)S(1)}, u32[]{:S(2)}, u32[]{:S(2)}) collective-permute-start(bf16[2,4,160,128]{3,2,1,0:T(8,128)(2,1)S(1)} %get-tuple-element.15), channel_id=1, source_target_pairs={{0,4},{4,0},{1,5},{5,1},{2,6},{6,2},{3,7},{7,3},{8,12},{12,8},{9,1... | collective-permute-start | bytes 983048 | tf_op jit(solution)/shard_map/ppermute | solution.py:249
  16.9 7.3 %collective-permute-start.1 = (bf16[4,160,128]{2,1,0:T(8,128)(2,1)S(1)}, bf16[4,160,128]{2,1,0:T(8,128)(2,1)S(1)}, u32[]{:S(2)}, u32[]{:S(2)}) collective-permute-start(bf16[4,160,128]{2,1,0:T(8,128)(2,1)S(1)} %get-tuple-element.19), channel_id=1, source_target_pairs={{0,8},{8,16},{16,24},{24,32},{32,40},{40,48},{48,56},{56,64},{64,7... | collective-permute-start | bytes 491528 | tf_op jit(solution)/shard_map/ppermute | solution.py:245
  18.2 7.4 %collective-permute-start.2 = (bf16[4,160,128]{2,1,0:T(8,128)(2,1)S(1)}, bf16[4,160,128]{2,1,0:T(8,128)(2,1)S(1)}, u32[]{:S(2)}, u32[]{:S(2)}) collective-permute-start(bf16[4,160,128]{2,1,0:T(8,128)(2,1)S(1)} %get-tuple-element.20), channel_id=1, source_target_pairs={{8,0},{16,8},{24,16},{32,24},{40,32},{48,40},{56,48},{64,56},{72,6... | collective-permute-start | bytes 491528 | tf_op jit(solution)/shard_map/ppermute | solution.py:245

commit v3 on v2

--- a/solution.py
+++ b/solution.py
@@ -121,10 +121,12 @@
     info[2 * BLK_DEV] = first - base
     info[2 * BLK_DEV + 1] = last + 1 - base
     info[2 * BLK_DEV + 2] = rep
+    info[2 * BLK_DEV + 3] = device % 2
 
     def store(pair, a, b):
         group, at = divmod(pair, SHIFT_MOST // 2)
-        outs = [out.at[group, part] for out in (kept, given) for part in range(HALF)]
+        turn = group ^ (device % 2)
+        outs = [out.at[turn, part] for out in (kept, given) for part in range(HALF)]
         interleaved(a, b, columns, outs, at * 2 * columns)
 
     lower.wait()
@@ -206,26 +208,28 @@
     )(pltpu.with_memory_space_constraint(info, pltpu.SMEM), tiles, weights)
 
 
-def combine_kernel(info, pieces, left, right, chip):
-    size, edge = chip.shape[1], left.shape[1]
+def combine_kernel(info, pieces, first, second, chip):
+    size, edge = pieces.shape[2], first.shape[1]
     columns = edge // SHIFT_MOST
     row = lax.broadcasted_iota(jnp.int32, (edge, chip.shape[2]), 0)
     below = row < info[2 * BLK_DEV] * columns
     above = row >= (info[2 * BLK_DEV + 1] - (BLK_DEV - SHIFT_MOST)) * columns
+    is_odd = info[2 * BLK_DEV + 3] == 1
     for part in range(HALF):
         for mask, other, rows in (
-            (below, left, slice(0, edge)),
+            (below, (first, second), slice(0, edge)),
             (None, None, slice(edge, size - edge)),
-            (above, right, slice(size - edge, size)),
+            (above, (second, first), slice(size - edge, size)),
         ):
             value = pieces[0, part, rows, :].astype(jnp.float32)
             value = value + pieces[1, part, rows, :].astype(jnp.float32)
             if mask is not None:
-                value = jnp.where(mask, other[part].astype(jnp.float32), value)
+                even, odd = (x[part].astype(jnp.float32) for x in other)
+                value = jnp.where(mask, jnp.where(is_odd, odd, even), value)
             chip[part, rows, :] = value.astype(chip.dtype)
 
 
-def combine(info, pieces, left, right):
+def combine(info, pieces, first, second):
     vmem = pl.BlockSpec(memory_space=pltpu.VMEM)
     return pl.pallas_call(
         combine_kernel,
@@ -236,13 +240,15 @@
             flops=pieces.size, bytes_accessed=4 * pieces.size, transcendentals=0
         ),
         compiler_params=pltpu.CompilerParams(vmem_limit_bytes=8 * MIB),
-    )(pltpu.with_memory_space_constraint(info, pltpu.SMEM), pieces, left, right)
-
-
-def shifted(block, axis, distance):
-    count = lax.axis_size(axis)
-    route = [(i, i + distance) for i in range(count) if 0 <= i + distance < count]
-    return lax.ppermute(block, axis, route)
+    )(pltpu.with_memory_space_constraint(info, pltpu.SMEM), pieces, first, second)
+
+
+def exchanged(block, turn):
+    route = []
+    for upper in range(1, lax.axis_size("blk")):
+        if upper % 2 == turn:
+            route += [(upper - 1, upper), (upper, upper - 1)]
+    return lax.ppermute(block, "blk", route)
 
 
 def swapped(block):
@@ -256,16 +262,16 @@
     kept_out, given_out, tiles, weights, info = outward(sector_tiles, offsets, t2_source, weights)
     taken_out = swapped(given_out)
     partial = own(info, tiles, weights)
-    leftward, rightward = (
+    first, second = (
         (kept_out[i].astype(jnp.float32) + taken_out[i].astype(jnp.float32)).astype(jnp.bfloat16)
         for i in range(2)
     )
-    leftward, rightward, partial = lax.optimization_barrier((leftward, rightward, partial))
-    from_left = shifted(rightward, "blk", 1)
-    from_right = shifted(leftward, "blk", -1)
+    first, second, partial = lax.optimization_barrier((first, second, partial))
+    first = exchanged(first, 0)
+    second = exchanged(second, 1)
 
     pieces = lax.all_to_all(partial, "rep", 0, 0, tiled=True)
-    chip = combine(info, pieces, from_left, from_right)
+    chip = combine(info, pieces, first, second)
     chunks = lax.all_to_all(chip, "slab", 0, 0, tiled=True)
     a, b, c, d = (chunks[i].astype(jnp.float32) for i in range(HALF))
     total = ((a + b) + (c + d)).astype(jnp.bfloat16)

time: 39.3 us -> 38.7 us (0.985)
  waiting for transfers between devices: 1.42 us -> 0.79 us
    ppermute x2, waiting for transfers between devices: 1.42 us -> 0.79 us  [exchanged(): return lax.ppermute(block, 'blk', route)]
where the time goes in v3:
time: 38.7 us; the launch traced here: 38.2 us
  blocking collectives  16.9 us (44%)
  starting transfers between devices  15 us (39%)
  Pallas kernels  4.61 us (12%)
  other arithmetic  0.84 us (2%)
  waiting for transfers between devices  0.79 us (2%)
    ppermute x1, starting transfers between devices, swapped(): return lax.ppermute(block, 'rep', [(0, 1), (1, 0)])  12.4 us
    all_to_all x1, blocking collectives, per_device(): chunks = lax.all_to_all(chip, 'slab', 0, 0, tiled=True)  12.2 us
    all_to_all x1, blocking collectives, per_device(): pieces = lax.all_to_all(partial, 'rep', 0, 0, tiled=True)  4.69 us
    pallas_call x1, Pallas kernels, outward(): pl.pallas_call(outward_kernel, out_shape=[out, out, jax.ShapeDtypeStruct(...  3.05 us
    ppermute x2, starting transfers between devices, exchanged(): return lax.ppermute(block, 'blk', route)  2.59 us
    pallas_call x1, Pallas kernels, own(): pl.pallas_call(own_kernel, out_shape=jax.ShapeDtypeStruct((2, HALF, BLK_D...  1.3 us
    ppermute x2, waiting for transfers between devices, exchanged(): return lax.ppermute(block, 'blk', route)  0.79 us
  transfers between devices with their start and end apart: 3, of which 1 were waited for; matrix products, arithmetic and copies ran while one was open for 0% of the time, Pallas kernels for 3%

profile of v3, /device:TPU:1, one launch (start us, length us, event | category | flops | bytes accessed | tf_op | source)
XLA Modules:
  0.0 38.2 jit_solution(13076637551223754152)
XLA Ops:
  0.0 3.0 %shard_map.46 = (bf16[2,4,160,128]{3,2,1,0:T(8,128)(2,1)S(1)}, bf16[2,4,160,128]{3,2,1,0:T(8,128)(2,1)S(1)}, bf16[20,128,640]{2,1,0:T(8,128)(2,1)S(1)}, bf16[8,320,640]{2,1,0:T(8,128)(2,1)S(1)}, s32[128]{0:T(128)S(4)}) custom-call(s32[8]{0:T(128)} %sector_tiles.1, s32[2,96]{1,0:T(2,128)} %bitcast.10, bf16[24,128,640]{2,1,0:T(8,128)(2,1)} %t2.1, ...), custom_call_target="tpu_custom_call" | custom-call | flops 419430400 | bytes 3932160 | tf_op jit(solution)/shard_map/pallas_call | solution.py:149
  3.1 12.4 %collective-permute-start = (bf16[2,4,160,128]{3,2,1,0:T(8,128)(2,1)S(1)}, bf16[2,4,160,128]{3,2,1,0:T(8,128)(2,1)S(1)}, u32[]{:S(2)}, u32[]{:S(2)}) collective-permute-start(bf16[2,4,160,128]{3,2,1,0:T(8,128)(2,1)S(1)} %get-tuple-element.15), channel_id=1, source_target_pairs={{0,4},{4,0},{1,5},{5,1},{2,6},{6,2},{3,7},{7,3},{8,12},{12,8},{9,1... | collective-permute-start | bytes 983048 | tf_op jit(solution)/shard_map/ppermute | solution.py:255
  15.5 1.3 %shard_map.47 = bf16[2,4,640,128]{3,2,1,0:T(8,128)(2,1)S(1)} custom-call(s32[128]{0:T(128)S(4)} %get-tuple-element.13.info, bf16[20,128,640]{2,1,0:T(8,128)(2,1)S(1)} %get-tuple-element.16.tiles, bf16[8,320,640]{2,1,0:T(8,128)(2,1)S(1)} %get-tuple-element.17.weights), custom_call_target="tpu_custom_call" | custom-call | flops 838860800 | bytes 4587520 | tf_op jit(solution)/shard_map/pallas_call | solution.py:195
  16.8 0.0 collective-permute-done
  16.8 0.1 fusion.1
  16.9 0.7 %collective-permute-start.1 = (bf16[4,160,128]{2,1,0:T(8,128)(2,1)S(1)}, bf16[4,160,128]{2,1,0:T(8,128)(2,1)S(1)}, u32[]{:S(2)}, u32[]{:S(2)}) collective-permute-start(bf16[4,160,128]{2,1,0:T(8,128)(2,1)S(1)} %get-tuple-element.19), channel_id=1, source_target_pairs={{8,16},{16,8},{24,32},{32,24},{40,48},{48,40},{56,64},{64,56},{72,... | collective-permute-start | bytes 491528 | tf_op jit(solution)/shard_map/ppermute | solution.py:251
  17.6 1.9 %collective-permute-start.2 = (bf16[4,160,128]{2,1,0:T(8,128)(2,1)S(1)}, bf16[4,160,128]{2,1,0:T(8,128)(2,1)S(1)}, u32[]{:S(2)}, u32[]{:S(2)}) collective-permute-start(bf16[4,160,128]{2,1,0:T(8,128)(2,1)S(1)} %get-tuple-element.20), channel_id=1, source_target_pairs={{0,8},{8,0},{16,24},{24,16},{32,40},{40,32},{48,56},{56,48},{64,72... | collective-permute-start | bytes 491528 | tf_op jit(solution)/shard_map/ppermute | solution.py:251
  19.5 4.7 %all_to_all.10.pieces = bf16[2,4,640,128]{3,2,1,0:T(8,128)(2,1)S(1)} all-to-all(bf16[2,4,640,128]{3,2,1,0:T(8,128)(2,1)S(1)} %shard_map.47), channel_id=1, replica_groups=mesh['blk'=96,'rep'=2,'slab'=4] {'rep'}, dimensions={0} | all-to-all | bytes 2621440 | tf_op jit(solution)/shard_map/all_to_all | solution.py:273
  24.2 0.0 collective-permute-done.1.first
  24.2 0.8 %collective-permute-done.2.second = bf16[4,160,128]{2,1,0:T(8,128)(2,1)S(1)} collective-permute-done((bf16[4,160,128]{2,1,0:T(8,128)(2,1)S(1)}, bf16[4,160,128]{2,1,0:T(8,128)(2,1)S(1)}, u32[]{:S(2)}, u32[]{:S(2)}) %collective-permute-start.2) | collective-permute-done | bytes 163872 | tf_op jit(solution)/shard_map/ppermute | solution.py:251
  25.0 0.3 shard_map.48
  25.3 12.2 %all_to_all.11 = bf16[4,640,128]{2,1,0:T(8,128)(2,1)S(1)} all-to-all(bf16[4,640,128]{2,1,0:T(8,128)(2,1)S(1)} %shard_map.48), channel_id=1, replica_groups=mesh['blk'=96,'rep'=2,'slab'=4] {'slab'}, dimensions={0} | all-to-all | bytes 1310720 | tf_op jit(solution)/shard_map/all_to_all | solution.py:275
  37.5 0.8 %add_convert_fusion = bf16[1,640,128]{2,1,0:T(8,128)(2,1)} fusion(bf16[4,640,128]{2,1,0:T(8,128)(2,1)S(1)} %all_to_all.11), kind=kLoop, calls=%fused_computation | loop fusion | flops 655360 | bytes 819200 | tf_op jit(solution)/shard_map/convert_element_type | solution.py:277
Async XLA Ops:
  3.1 13.7 %collective-permute-start = (bf16[2,4,160,128]{3,2,1,0:T(8,128)(2,1)S(1)}, bf16[2,4,160,128]{3,2,1,0:T(8,128)(2,1)S(1)}, u32[]{:S(2)}, u32[]{:S(2)}) collective-permute-start(bf16[2,4,160,128]{3,2,1,0:T(8,128)(2,1)S(1)} %get-tuple-element.15), channel_id=1, source_target_pairs={{0,4},{4,0},{1,5},{5,1},{2,6},{6,2},{3,7},{7,3},{8,12},{12,8},{9,1... | collective-permute-start | bytes 983048 | tf_op jit(solution)/shard_map/ppermute | solution.py:255
  16.9 7.3 %collective-permute-start.1 = (bf16[4,160,128]{2,1,0:T(8,128)(2,1)S(1)}, bf16[4,160,128]{2,1,0:T(8,128)(2,1)S(1)}, u32[]{:S(2)}, u32[]{:S(2)}) collective-permute-start(bf16[4,160,128]{2,1,0:T(8,128)(2,1)S(1)} %get-tuple-element.19), channel_id=1, source_target_pairs={{8,16},{16,8},{24,32},{32,24},{40,48},{48,40},{56,64},{64,56},{72,... | collective-permute-start | bytes 491528 | tf_op jit(solution)/shard_map/ppermute | solution.py:251
  17.6 7.4 %collective-permute-start.2 = (bf16[4,160,128]{2,1,0:T(8,128)(2,1)S(1)}, bf16[4,160,128]{2,1,0:T(8,128)(2,1)S(1)}, u32[]{:S(2)}, u32[]{:S(2)}) collective-permute-start(bf16[4,160,128]{2,1,0:T(8,128)(2,1)S(1)} %get-tuple-element.20), channel_id=1, source_target_pairs={{0,8},{8,0},{16,24},{24,16},{32,40},{40,32},{48,56},{56,48},{64,72... | collective-permute-start | bytes 491528 | tf_op jit(solution)/shard_map/ppermute | solution.py:251

commit v4 on v3

--- a/solution.py
+++ b/solution.py
@@ -1,3 +1,5 @@
+import functools
+
 import jax
 import jax.numpy as jnp
 from jax import lax
@@ -10,6 +12,7 @@
 PARTS = 8
 HALF = 4
 MIB = 1024 * 1024
+EARLY = 6
 
 
 def product_pairs(weights, sectors, tiles, store):
@@ -57,7 +60,17 @@
     lower = pltpu.make_async_copy(
         t2.at[pl.ds(0, SHIFT_MOST)], tiles.at[pl.ds(0, SHIFT_MOST)], tile_sems.at[0]
     )
-    for copy in small + [lower]:
+    middle = SHIFT_MOST + EARLY
+    others = [
+        pltpu.make_async_copy(
+            t2.at[pl.ds(start, end - start)], tiles.at[pl.ds(start, end - start)], sem
+        )
+        for start, end, sem in (
+            (SHIFT_MOST, middle, tile_sems.at[2]),
+            (middle, reach, tile_sems.at[3]),
+        )
+    ]
+    for copy in small + [lower, others[0]]:
         copy.start()
     for copy in small:
         copy.wait()
@@ -93,13 +106,10 @@
         upper,
         tile_sems.at[1],
     )
-    others = pltpu.make_async_copy(
-        t2.at[pl.ds(SHIFT_MOST, reach - SHIFT_MOST)],
-        tiles.at[pl.ds(SHIFT_MOST, reach - SHIFT_MOST)],
-        tile_sems.at[2],
-    )
-    above.start()
-    others.start()
+    has_left = first < base
+    has_right = last >= base + BLK_DEV
+    pl.when(has_right)(above.start)
+    others[1].start()
 
     def sector_of(block):
         held = jnp.clip(block, first, last)
@@ -123,17 +133,28 @@
     info[2 * BLK_DEV + 2] = rep
     info[2 * BLK_DEV + 3] = device % 2
 
-    def store(pair, a, b):
-        group, at = divmod(pair, SHIFT_MOST // 2)
+    def store(group, pair, a, b):
         turn = group ^ (device % 2)
         outs = [out.at[turn, part] for out in (kept, given) for part in range(HALF)]
-        interleaved(a, b, columns, outs, at * 2 * columns)
+        interleaved(a, b, columns, outs, pair * 2 * columns)
 
     lower.wait()
     each_weight(lambda copy: copy.wait())
-    above.wait()
-    product_pairs(weights, sectors, edges, store)
-    others.wait()
+
+
+    @pl.when(has_left)
+    def _():
+        low = slice(0, SHIFT_MOST)
+        product_pairs(weights, sectors[low], edges[low], functools.partial(store, 0))
+
+    @pl.when(has_right)
+    def _():
+        above.wait()
+        high = slice(SHIFT_MOST, 2 * SHIFT_MOST)
+        product_pairs(weights, sectors[high], edges[high], functools.partial(store, 1))
+
+    for copy in others:
+        copy.wait()
 
 
 def outward(sector_tiles, offsets, t2, integrals):
@@ -163,7 +184,7 @@
             pltpu.VMEM((SHIFT_MOST, rows, depth), t2.dtype),
             pltpu.SemaphoreType.DMA(()),
             pltpu.SemaphoreType.DMA(()),
-            pltpu.SemaphoreType.DMA((3,)),
+            pltpu.SemaphoreType.DMA((4,)),
             pltpu.SemaphoreType.DMA((sectors, 2)),
         ],
         cost_estimate=pl.CostEstimate(
@@ -243,6 +264,35 @@
     )(pltpu.with_memory_space_constraint(info, pltpu.SMEM), pieces, first, second)
 
 
+def sum_kernel(chunks, out, total, sems):
+    pieces = sems.shape[0]
+    size = total.shape[0] // pieces
+    copies = []
+    for i in range(pieces):
+        rows = slice(i * size, (i + 1) * size)
+        a, b, c, d = (chunks[k, rows, :].astype(jnp.float32) for k in range(HALF))
+        total[rows, :] = ((a + b) + (c + d)).astype(total.dtype)
+        copies.append(pltpu.make_async_copy(total.at[rows], out.at[rows], sems.at[i]))
+        copies[-1].start()
+    for copy in copies:
+        copy.wait()
+
+
+def add_up(chunks):
+    _, rows, lanes = chunks.shape
+    return pl.pallas_call(
+        sum_kernel,
+        out_shape=jax.ShapeDtypeStruct((rows, lanes), chunks.dtype),
+        in_specs=[pl.BlockSpec(memory_space=pltpu.VMEM)],
+        out_specs=pl.BlockSpec(memory_space=pltpu.HBM),
+        scratch_shapes=[
+            pltpu.VMEM((rows, lanes), chunks.dtype),
+            pltpu.SemaphoreType.DMA((4,)),
+        ],
+        compiler_params=pltpu.CompilerParams(vmem_limit_bytes=8 * MIB),
+    )(chunks)
+
+
 def exchanged(block, turn):
     route = []
     for upper in range(1, lax.axis_size("blk")):
@@ -273,8 +323,7 @@
     pieces = lax.all_to_all(partial, "rep", 0, 0, tiled=True)
     chip = combine(info, pieces, first, second)
     chunks = lax.all_to_all(chip, "slab", 0, 0, tiled=True)
-    a, b, c, d = (chunks[i].astype(jnp.float32) for i in range(HALF))
-    total = ((a + b) + (c + d)).astype(jnp.bfloat16)
+    total = add_up(chunks)
     return jnp.swapaxes(total.reshape(BLK_DEV, -1, total.shape[1]), 1, 2)
 
 

time: 38.7 us -> 38.8 us (level)
  other arithmetic: 0.84 us -> 0.09 us
  Pallas kernels: 4.61 us -> 5.16 us
    convert_element_type x1 -> x0, other arithmetic: 0.75 us -> none  [per_device(): total = (a + b + (c + d)).astype(jnp.bfloat16)]
    pallas_call x0 -> x1, Pallas kernels: none -> 0.73 us  [add_up(): pl.pallas_call(sum_kernel, out_shape=jax.ShapeDtypeStruct((rows, lanes),...]
where the time goes in v4:
time: 38.8 us; the launch traced here: 38 us
  blocking collectives  16.9 us (44%)
  starting transfers between devices  15 us (39%)
  Pallas kernels  5.16 us (13%)
  waiting for transfers between devices  0.79 us (2%)
    ppermute x1, starting transfers between devices, swapped(): return lax.ppermute(block, 'rep', [(0, 1), (1, 0)])  12.4 us
    all_to_all x1, blocking collectives, per_device(): chunks = lax.all_to_all(chip, 'slab', 0, 0, tiled=True)  12.2 us
    all_to_all x1, blocking collectives, per_device(): pieces = lax.all_to_all(partial, 'rep', 0, 0, tiled=True)  4.69 us
    pallas_call x1, Pallas kernels, outward(): pl.pallas_call(outward_kernel, out_shape=[out, out, jax.ShapeDtypeStruct(...  2.86 us
    ppermute x2, starting transfers between devices, exchanged(): return lax.ppermute(block, 'blk', route)  2.59 us
    pallas_call x1, Pallas kernels, own(): pl.pallas_call(own_kernel, out_shape=jax.ShapeDtypeStruct((2, HALF, BLK_D...  1.3 us
    ppermute x2, waiting for transfers between devices, exchanged(): return lax.ppermute(block, 'blk', route)  0.79 us
  transfers between devices with their start and end apart: 3, of which 1 were waited for; matrix products, arithmetic and copies ran while one was open for 0% of the time, Pallas kernels for 3%

profile of v4, /device:TPU:1, one launch (start us, length us, event | category | flops | bytes accessed | tf_op | source)
XLA Modules:
  0.0 38.0 jit_solution(11651980893403327034)
XLA Ops:
  0.0 2.9 %shard_map.46 = (bf16[2,4,160,128]{3,2,1,0:T(8,128)(2,1)S(1)}, bf16[2,4,160,128]{3,2,1,0:T(8,128)(2,1)S(1)}, bf16[20,128,640]{2,1,0:T(8,128)(2,1)S(1)}, bf16[8,320,640]{2,1,0:T(8,128)(2,1)S(1)}, s32[128]{0:T(128)S(4)}) custom-call(s32[8]{0:T(128)} %sector_tiles.1, s32[2,96]{1,0:T(2,128)} %bitcast.10, bf16[24,128,640]{2,1,0:T(8,128)(2,1)} %t2.1, ...), custom_call_target="tpu_custom_call" | custom-call | flops 419430400 | bytes 3932160 | tf_op jit(solution)/shard_map/pallas_call | solution.py:170
  2.9 12.4 %collective-permute-start = (bf16[2,4,160,128]{3,2,1,0:T(8,128)(2,1)S(1)}, bf16[2,4,160,128]{3,2,1,0:T(8,128)(2,1)S(1)}, u32[]{:S(2)}, u32[]{:S(2)}) collective-permute-start(bf16[2,4,160,128]{3,2,1,0:T(8,128)(2,1)S(1)} %get-tuple-element.15), channel_id=1, source_target_pairs={{0,4},{4,0},{1,5},{5,1},{2,6},{6,2},{3,7},{7,3},{8,12},{12,8},{9,1... | collective-permute-start | bytes 983048 | tf_op jit(solution)/shard_map/ppermute | solution.py:305
  15.3 1.3 %shard_map.47 = bf16[2,4,640,128]{3,2,1,0:T(8,128)(2,1)S(1)} custom-call(s32[128]{0:T(128)S(4)} %get-tuple-element.13.info, bf16[20,128,640]{2,1,0:T(8,128)(2,1)S(1)} %get-tuple-element.16.tiles, bf16[8,320,640]{2,1,0:T(8,128)(2,1)S(1)} %get-tuple-element.17.weights), custom_call_target="tpu_custom_call" | custom-call | flops 838860800 | bytes 4587520 | tf_op jit(solution)/shard_map/pallas_call | solution.py:216
  16.6 0.0 collective-permute-done
  16.6 0.1 fusion.1
  16.7 0.7 %collective-permute-start.1 = (bf16[4,160,128]{2,1,0:T(8,128)(2,1)S(1)}, bf16[4,160,128]{2,1,0:T(8,128)(2,1)S(1)}, u32[]{:S(2)}, u32[]{:S(2)}) collective-permute-start(bf16[4,160,128]{2,1,0:T(8,128)(2,1)S(1)} %get-tuple-element.19), channel_id=1, source_target_pairs={{8,16},{16,8},{24,32},{32,24},{40,48},{48,40},{56,64},{64,56},{72,... | collective-permute-start | bytes 491528 | tf_op jit(solution)/shard_map/ppermute | solution.py:301
  17.4 1.9 %collective-permute-start.2 = (bf16[4,160,128]{2,1,0:T(8,128)(2,1)S(1)}, bf16[4,160,128]{2,1,0:T(8,128)(2,1)S(1)}, u32[]{:S(2)}, u32[]{:S(2)}) collective-permute-start(bf16[4,160,128]{2,1,0:T(8,128)(2,1)S(1)} %get-tuple-element.20), channel_id=1, source_target_pairs={{0,8},{8,0},{16,24},{24,16},{32,40},{40,32},{48,56},{56,48},{64,72... | collective-permute-start | bytes 491528 | tf_op jit(solution)/shard_map/ppermute | solution.py:301
  19.3 4.7 %all_to_all.10.pieces = bf16[2,4,640,128]{3,2,1,0:T(8,128)(2,1)S(1)} all-to-all(bf16[2,4,640,128]{3,2,1,0:T(8,128)(2,1)S(1)} %shard_map.47), channel_id=1, replica_groups=mesh['blk'=96,'rep'=2,'slab'=4] {'rep'}, dimensions={0} | all-to-all | bytes 2621440 | tf_op jit(solution)/shard_map/all_to_all | solution.py:323
  24.0 0.0 collective-permute-done.1.first
  24.0 0.8 %collective-permute-done.2.second = bf16[4,160,128]{2,1,0:T(8,128)(2,1)S(1)} collective-permute-done((bf16[4,160,128]{2,1,0:T(8,128)(2,1)S(1)}, bf16[4,160,128]{2,1,0:T(8,128)(2,1)S(1)}, u32[]{:S(2)}, u32[]{:S(2)}) %collective-permute-start.2) | collective-permute-done | bytes 163872 | tf_op jit(solution)/shard_map/ppermute | solution.py:301
  24.8 0.3 shard_map.48
  25.1 12.2 %all_to_all.11.chunks = bf16[4,640,128]{2,1,0:T(8,128)(2,1)S(1)} all-to-all(bf16[4,640,128]{2,1,0:T(8,128)(2,1)S(1)} %shard_map.48), channel_id=1, replica_groups=mesh['blk'=96,'rep'=2,'slab'=4] {'slab'}, dimensions={0} | all-to-all | bytes 1310720 | tf_op jit(solution)/shard_map/all_to_all | solution.py:325
  37.3 0.7 %shard_map.49 = bf16[640,128]{1,0:T(8,128)(2,1)} custom-call(bf16[4,640,128]{2,1,0:T(8,128)(2,1)S(1)} %all_to_all.11.chunks), custom_call_target="tpu_custom_call" | custom-call | tf_op jit(solution)/shard_map/pallas_call | solution.py:283
Async XLA Ops:
  2.9 13.7 %collective-permute-start = (bf16[2,4,160,128]{3,2,1,0:T(8,128)(2,1)S(1)}, bf16[2,4,160,128]{3,2,1,0:T(8,128)(2,1)S(1)}, u32[]{:S(2)}, u32[]{:S(2)}) collective-permute-start(bf16[2,4,160,128]{3,2,1,0:T(8,128)(2,1)S(1)} %get-tuple-element.15), channel_id=1, source_target_pairs={{0,4},{4,0},{1,5},{5,1},{2,6},{6,2},{3,7},{7,3},{8,12},{12,8},{9,1... | collective-permute-start | bytes 983048 | tf_op jit(solution)/shard_map/ppermute | solution.py:305
  16.7 7.3 %collective-permute-start.1 = (bf16[4,160,128]{2,1,0:T(8,128)(2,1)S(1)}, bf16[4,160,128]{2,1,0:T(8,128)(2,1)S(1)}, u32[]{:S(2)}, u32[]{:S(2)}) collective-permute-start(bf16[4,160,128]{2,1,0:T(8,128)(2,1)S(1)} %get-tuple-element.19), channel_id=1, source_target_pairs={{8,16},{16,8},{24,32},{32,24},{40,48},{48,40},{56,64},{64,56},{72,... | collective-permute-start | bytes 491528 | tf_op jit(solution)/shard_map/ppermute | solution.py:301
  17.4 7.4 %collective-permute-start.2 = (bf16[4,160,128]{2,1,0:T(8,128)(2,1)S(1)}, bf16[4,160,128]{2,1,0:T(8,128)(2,1)S(1)}, u32[]{:S(2)}, u32[]{:S(2)}) collective-permute-start(bf16[4,160,128]{2,1,0:T(8,128)(2,1)S(1)} %get-tuple-element.20), channel_id=1, source_target_pairs={{0,8},{8,0},{16,24},{24,16},{32,40},{40,32},{48,56},{56,48},{64,72... | collective-permute-start | bytes 491528 | tf_op jit(solution)/shard_map/ppermute | solution.py:301

commit v5 on v4

--- a/solution.py
+++ b/solution.py
@@ -229,25 +229,32 @@
     )(pltpu.with_memory_space_constraint(info, pltpu.SMEM), tiles, weights)
 
 
-def combine_kernel(info, pieces, first, second, chip):
+def combine_kernel(info, first, second, pieces, chip):
     size, edge = pieces.shape[2], first.shape[1]
     columns = edge // SHIFT_MOST
-    row = lax.broadcasted_iota(jnp.int32, (edge, chip.shape[2]), 0)
+    row = lax.broadcasted_iota(jnp.int32, (edge, pieces.shape[3]), 0)
     below = row < info[2 * BLK_DEV] * columns
     above = row >= (info[2 * BLK_DEV + 1] - (BLK_DEV - SHIFT_MOST)) * columns
-    is_odd = info[2 * BLK_DEV + 3] == 1
+
+    def own(part, rows):
+        value = pieces[0, part, rows, :].astype(jnp.float32)
+        return value + pieces[1, part, rows, :].astype(jnp.float32)
+
     for part in range(HALF):
-        for mask, other, rows in (
-            (below, (first, second), slice(0, edge)),
-            (None, None, slice(edge, size - edge)),
-            (above, (second, first), slice(size - edge, size)),
-        ):
-            value = pieces[0, part, rows, :].astype(jnp.float32)
-            value = value + pieces[1, part, rows, :].astype(jnp.float32)
-            if mask is not None:
-                even, odd = (x[part].astype(jnp.float32) for x in other)
-                value = jnp.where(mask, jnp.where(is_odd, odd, even), value)
-            chip[part, rows, :] = value.astype(chip.dtype)
+        rows = slice(edge, size - edge)
+        chip[part, rows, :] = own(part, rows).astype(chip.dtype)
+
+    for odd, (left, right) in enumerate(((first, second), (second, first))):
+
+        @pl.when(info[2 * BLK_DEV + 3] == odd)
+        def _():
+            for part in range(HALF):
+                for mask, other, rows in (
+                    (below, left, slice(0, edge)),
+                    (above, right, slice(size - edge, size)),
+                ):
+                    value = jnp.where(mask, other[part].astype(jnp.float32), own(part, rows))
+                    chip[part, rows, :] = value.astype(chip.dtype)
 
 
 def combine(info, pieces, first, second):
@@ -261,7 +268,7 @@
             flops=pieces.size, bytes_accessed=4 * pieces.size, transcendentals=0
         ),
         compiler_params=pltpu.CompilerParams(vmem_limit_bytes=8 * MIB),
-    )(pltpu.with_memory_space_constraint(info, pltpu.SMEM), pieces, first, second)
+    )(pltpu.with_memory_space_constraint(info, pltpu.SMEM), first, second, pieces)
 
 
 def sum_kernel(chunks, out, total, sems):

time: 38.8 us -> 38.5 us (level)
  no operation moved by 1% of the time
where the time goes in v5:
time: 38.5 us; the launch traced here: 38 us
  blocking collectives  16.9 us (44%)
  starting transfers between devices  15 us (39%)
  Pallas kernels  5.13 us (13%)
  waiting for transfers between devices  0.79 us (2%)
    ppermute x1, starting transfers between devices, swapped(): return lax.ppermute(block, 'rep', [(0, 1), (1, 0)])  12.4 us
    all_to_all x1, blocking collectives, per_device(): chunks = lax.all_to_all(chip, 'slab', 0, 0, tiled=True)  12.2 us
    all_to_all x1, blocking collectives, per_device(): pieces = lax.all_to_all(partial, 'rep', 0, 0, tiled=True)  4.69 us
    pallas_call x1, Pallas kernels, outward(): pl.pallas_call(outward_kernel, out_shape=[out, out, jax.ShapeDtypeStruct(...  2.86 us
    ppermute x2, starting transfers between devices, exchanged(): return lax.ppermute(block, 'blk', route)  2.59 us
    pallas_call x1, Pallas kernels, own(): pl.pallas_call(own_kernel, out_shape=jax.ShapeDtypeStruct((2, HALF, BLK_D...  1.3 us
    ppermute x2, waiting for transfers between devices, exchanged(): return lax.ppermute(block, 'blk', route)  0.79 us
  transfers between devices with their start and end apart: 3, of which 1 were waited for; matrix products, arithmetic and copies ran while one was open for 0% of the time, Pallas kernels for 3%

profile of v5, /device:TPU:1, one launch (start us, length us, event | category | flops | bytes accessed | tf_op | source)
XLA Modules:
  0.0 38.0 jit_solution(8101266700787710937)
XLA Ops:
  0.0 2.9 %shard_map.46 = (bf16[2,4,160,128]{3,2,1,0:T(8,128)(2,1)S(1)}, bf16[2,4,160,128]{3,2,1,0:T(8,128)(2,1)S(1)}, bf16[20,128,640]{2,1,0:T(8,128)(2,1)S(1)}, bf16[8,320,640]{2,1,0:T(8,128)(2,1)S(1)}, s32[128]{0:T(128)S(4)}) custom-call(s32[8]{0:T(128)} %sector_tiles.1, s32[2,96]{1,0:T(2,128)} %bitcast.10, bf16[24,128,640]{2,1,0:T(8,128)(2,1)} %t2.1, ...), custom_call_target="tpu_custom_call" | custom-call | flops 419430400 | bytes 3932160 | tf_op jit(solution)/shard_map/pallas_call | solution.py:170
  2.9 12.4 %collective-permute-start = (bf16[2,4,160,128]{3,2,1,0:T(8,128)(2,1)S(1)}, bf16[2,4,160,128]{3,2,1,0:T(8,128)(2,1)S(1)}, u32[]{:S(2)}, u32[]{:S(2)}) collective-permute-start(bf16[2,4,160,128]{3,2,1,0:T(8,128)(2,1)S(1)} %get-tuple-element.15), channel_id=1, source_target_pairs={{0,4},{4,0},{1,5},{5,1},{2,6},{6,2},{3,7},{7,3},{8,12},{12,8},{9,1... | collective-permute-start | bytes 983048 | tf_op jit(solution)/shard_map/ppermute | solution.py:312
  15.3 1.3 %shard_map.47 = bf16[2,4,640,128]{3,2,1,0:T(8,128)(2,1)S(1)} custom-call(s32[128]{0:T(128)S(4)} %get-tuple-element.13.info, bf16[20,128,640]{2,1,0:T(8,128)(2,1)S(1)} %get-tuple-element.16.tiles, bf16[8,320,640]{2,1,0:T(8,128)(2,1)S(1)} %get-tuple-element.17.weights), custom_call_target="tpu_custom_call" | custom-call | flops 838860800 | bytes 4587520 | tf_op jit(solution)/shard_map/pallas_call | solution.py:216
  16.6 0.0 collective-permute-done
  16.6 0.1 fusion.1
  16.7 0.7 %collective-permute-start.1 = (bf16[4,160,128]{2,1,0:T(8,128)(2,1)S(1)}, bf16[4,160,128]{2,1,0:T(8,128)(2,1)S(1)}, u32[]{:S(2)}, u32[]{:S(2)}) collective-permute-start(bf16[4,160,128]{2,1,0:T(8,128)(2,1)S(1)} %get-tuple-element.18), channel_id=1, source_target_pairs={{8,16},{16,8},{24,32},{32,24},{40,48},{48,40},{56,64},{64,56},{72,... | collective-permute-start | bytes 491528 | tf_op jit(solution)/shard_map/ppermute | solution.py:308
  17.4 1.9 %collective-permute-start.2 = (bf16[4,160,128]{2,1,0:T(8,128)(2,1)S(1)}, bf16[4,160,128]{2,1,0:T(8,128)(2,1)S(1)}, u32[]{:S(2)}, u32[]{:S(2)}) collective-permute-start(bf16[4,160,128]{2,1,0:T(8,128)(2,1)S(1)} %get-tuple-element.19), channel_id=1, source_target_pairs={{0,8},{8,0},{16,24},{24,16},{32,40},{40,32},{48,56},{56,48},{64,72... | collective-permute-start | bytes 491528 | tf_op jit(solution)/shard_map/ppermute | solution.py:308
  19.3 4.7 %all_to_all.10.pieces = bf16[2,4,640,128]{3,2,1,0:T(8,128)(2,1)S(1)} all-to-all(bf16[2,4,640,128]{3,2,1,0:T(8,128)(2,1)S(1)} %shard_map.47), channel_id=1, replica_groups=mesh['blk'=96,'rep'=2,'slab'=4] {'rep'}, dimensions={0} | all-to-all | bytes 2621440 | tf_op jit(solution)/shard_map/all_to_all | solution.py:330
  24.0 0.0 collective-permute-done.1.first
  24.0 0.8 %collective-permute-done.2.second = bf16[4,160,128]{2,1,0:T(8,128)(2,1)S(1)} collective-permute-done((bf16[4,160,128]{2,1,0:T(8,128)(2,1)S(1)}, bf16[4,160,128]{2,1,0:T(8,128)(2,1)S(1)}, u32[]{:S(2)}, u32[]{:S(2)}) %collective-permute-start.2) | collective-permute-done | bytes 163872 | tf_op jit(solution)/shard_map/ppermute | solution.py:308
  24.8 0.2 shard_map.48
  25.0 12.2 %all_to_all.11.chunks = bf16[4,640,128]{2,1,0:T(8,128)(2,1)S(1)} all-to-all(bf16[4,640,128]{2,1,0:T(8,128)(2,1)S(1)} %shard_map.48), channel_id=1, replica_groups=mesh['blk'=96,'rep'=2,'slab'=4] {'slab'}, dimensions={0} | all-to-all | bytes 1310720 | tf_op jit(solution)/shard_map/all_to_all | solution.py:332
  37.3 0.7 %shard_map.49 = bf16[640,128]{1,0:T(8,128)(2,1)} custom-call(bf16[4,640,128]{2,1,0:T(8,128)(2,1)S(1)} %all_to_all.11.chunks), custom_call_target="tpu_custom_call" | custom-call | tf_op jit(solution)/shard_map/pallas_call | solution.py:290
Async XLA Ops:
  2.9 13.7 %collective-permute-start = (bf16[2,4,160,128]{3,2,1,0:T(8,128)(2,1)S(1)}, bf16[2,4,160,128]{3,2,1,0:T(8,128)(2,1)S(1)}, u32[]{:S(2)}, u32[]{:S(2)}) collective-permute-start(bf16[2,4,160,128]{3,2,1,0:T(8,128)(2,1)S(1)} %get-tuple-element.15), channel_id=1, source_target_pairs={{0,4},{4,0},{1,5},{5,1},{2,6},{6,2},{3,7},{7,3},{8,12},{12,8},{9,1... | collective-permute-start | bytes 983048 | tf_op jit(solution)/shard_map/ppermute | solution.py:312
  16.7 7.3 %collective-permute-start.1 = (bf16[4,160,128]{2,1,0:T(8,128)(2,1)S(1)}, bf16[4,160,128]{2,1,0:T(8,128)(2,1)S(1)}, u32[]{:S(2)}, u32[]{:S(2)}) collective-permute-start(bf16[4,160,128]{2,1,0:T(8,128)(2,1)S(1)} %get-tuple-element.18), channel_id=1, source_target_pairs={{8,16},{16,8},{24,32},{32,24},{40,48},{48,40},{56,64},{64,56},{72,... | collective-permute-start | bytes 491528 | tf_op jit(solution)/shard_map/ppermute | solution.py:308
  17.4 7.4 %collective-permute-start.2 = (bf16[4,160,128]{2,1,0:T(8,128)(2,1)S(1)}, bf16[4,160,128]{2,1,0:T(8,128)(2,1)S(1)}, u32[]{:S(2)}, u32[]{:S(2)}) collective-permute-start(bf16[4,160,128]{2,1,0:T(8,128)(2,1)S(1)} %get-tuple-element.19), channel_id=1, source_target_pairs={{0,8},{8,0},{16,24},{24,16},{32,40},{40,32},{48,56},{56,48},{64,72... | collective-permute-start | bytes 491528 | tf_op jit(solution)/shard_map/ppermute | solution.py:308

commit v6 on v5

--- a/solution.py
+++ b/solution.py
@@ -294,7 +294,7 @@
         out_specs=pl.BlockSpec(memory_space=pltpu.HBM),
         scratch_shapes=[
             pltpu.VMEM((rows, lanes), chunks.dtype),
-            pltpu.SemaphoreType.DMA((4,)),
+            pltpu.SemaphoreType.DMA((2,)),
         ],
         compiler_params=pltpu.CompilerParams(vmem_limit_bytes=8 * MIB),
     )(chunks)

time: 38.5 us -> 38.5 us (level)
  no operation moved by 1% of the time
where the time goes in v6:
time: 38.5 us; the launch traced here: 38 us
  blocking collectives  16.9 us (44%)
  starting transfers between devices  15 us (39%)
  Pallas kernels  5.16 us (13%)
  waiting for transfers between devices  0.78 us (2%)
    ppermute x1, starting transfers between devices, swapped(): return lax.ppermute(block, 'rep', [(0, 1), (1, 0)])  12.4 us
    all_to_all x1, blocking collectives, per_device(): chunks = lax.all_to_all(chip, 'slab', 0, 0, tiled=True)  12.2 us
    all_to_all x1, blocking collectives, per_device(): pieces = lax.all_to_all(partial, 'rep', 0, 0, tiled=True)  4.7 us
    pallas_call x1, Pallas kernels, outward(): pl.pallas_call(outward_kernel, out_shape=[out, out, jax.ShapeDtypeStruct(...  2.9 us
    ppermute x2, starting transfers between devices, exchanged(): return lax.ppermute(block, 'blk', route)  2.59 us
    pallas_call x1, Pallas kernels, own(): pl.pallas_call(own_kernel, out_shape=jax.ShapeDtypeStruct((2, HALF, BLK_D...  1.3 us
    ppermute x2, waiting for transfers between devices, exchanged(): return lax.ppermute(block, 'blk', route)  0.78 us
  transfers between devices with their start and end apart: 3, of which 1 were waited for; matrix products, arithmetic and copies ran while one was open for 0% of the time, Pallas kernels for 3%

profile of v6, /device:TPU:1, one launch (start us, length us, event | category | flops | bytes accessed | tf_op | source)
XLA Modules:
  0.0 38.0 jit_solution(17514490306289170189)
XLA Ops:
  0.0 2.9 %shard_map.46 = (bf16[2,4,160,128]{3,2,1,0:T(8,128)(2,1)S(1)}, bf16[2,4,160,128]{3,2,1,0:T(8,128)(2,1)S(1)}, bf16[20,128,640]{2,1,0:T(8,128)(2,1)S(1)}, bf16[8,320,640]{2,1,0:T(8,128)(2,1)S(1)}, s32[128]{0:T(128)S(4)}) custom-call(s32[8]{0:T(128)} %sector_tiles.1, s32[2,96]{1,0:T(2,128)} %bitcast.10, bf16[24,128,640]{2,1,0:T(8,128)(2,1)} %t2.1, ...), custom_call_target="tpu_custom_call" | custom-call | flops 419430400 | bytes 3932160 | tf_op jit(solution)/shard_map/pallas_call | solution.py:170
  2.9 12.4 %collective-permute-start = (bf16[2,4,160,128]{3,2,1,0:T(8,128)(2,1)S(1)}, bf16[2,4,160,128]{3,2,1,0:T(8,128)(2,1)S(1)}, u32[]{:S(2)}, u32[]{:S(2)}) collective-permute-start(bf16[2,4,160,128]{3,2,1,0:T(8,128)(2,1)S(1)} %get-tuple-element.15), channel_id=1, source_target_pairs={{0,4},{4,0},{1,5},{5,1},{2,6},{6,2},{3,7},{7,3},{8,12},{12,8},{9,1... | collective-permute-start | bytes 983048 | tf_op jit(solution)/shard_map/ppermute | solution.py:312
  15.3 1.3 %shard_map.47 = bf16[2,4,640,128]{3,2,1,0:T(8,128)(2,1)S(1)} custom-call(s32[128]{0:T(128)S(4)} %get-tuple-element.13.info, bf16[20,128,640]{2,1,0:T(8,128)(2,1)S(1)} %get-tuple-element.16.tiles, bf16[8,320,640]{2,1,0:T(8,128)(2,1)S(1)} %get-tuple-element.17.weights), custom_call_target="tpu_custom_call" | custom-call | flops 838860800 | bytes 4587520 | tf_op jit(solution)/shard_map/pallas_call | solution.py:216
  16.6 0.0 collective-permute-done
  16.7 0.1 fusion.1
  16.8 0.7 %collective-permute-start.1 = (bf16[4,160,128]{2,1,0:T(8,128)(2,1)S(1)}, bf16[4,160,128]{2,1,0:T(8,128)(2,1)S(1)}, u32[]{:S(2)}, u32[]{:S(2)}) collective-permute-start(bf16[4,160,128]{2,1,0:T(8,128)(2,1)S(1)} %get-tuple-element.18), channel_id=1, source_target_pairs={{8,16},{16,8},{24,32},{32,24},{40,48},{48,40},{56,64},{64,56},{72,... | collective-permute-start | bytes 491528 | tf_op jit(solution)/shard_map/ppermute | solution.py:308
  17.4 1.9 %collective-permute-start.2 = (bf16[4,160,128]{2,1,0:T(8,128)(2,1)S(1)}, bf16[4,160,128]{2,1,0:T(8,128)(2,1)S(1)}, u32[]{:S(2)}, u32[]{:S(2)}) collective-permute-start(bf16[4,160,128]{2,1,0:T(8,128)(2,1)S(1)} %get-tuple-element.19), channel_id=1, source_target_pairs={{0,8},{8,0},{16,24},{24,16},{32,40},{40,32},{48,56},{56,48},{64,72... | collective-permute-start | bytes 491528 | tf_op jit(solution)/shard_map/ppermute | solution.py:308
  19.4 4.7 %all_to_all.10.pieces = bf16[2,4,640,128]{3,2,1,0:T(8,128)(2,1)S(1)} all-to-all(bf16[2,4,640,128]{3,2,1,0:T(8,128)(2,1)S(1)} %shard_map.47), channel_id=1, replica_groups=mesh['blk'=96,'rep'=2,'slab'=4] {'rep'}, dimensions={0} | all-to-all | bytes 2621440 | tf_op jit(solution)/shard_map/all_to_all | solution.py:330
  24.1 0.0 collective-permute-done.1.first
  24.1 0.8 %collective-permute-done.2.second = bf16[4,160,128]{2,1,0:T(8,128)(2,1)S(1)} collective-permute-done((bf16[4,160,128]{2,1,0:T(8,128)(2,1)S(1)}, bf16[4,160,128]{2,1,0:T(8,128)(2,1)S(1)}, u32[]{:S(2)}, u32[]{:S(2)}) %collective-permute-start.2) | collective-permute-done | bytes 163872 | tf_op jit(solution)/shard_map/ppermute | solution.py:308
  24.8 0.2 shard_map.48
  25.1 12.2 %all_to_all.11.chunks = bf16[4,640,128]{2,1,0:T(8,128)(2,1)S(1)} all-to-all(bf16[4,640,128]{2,1,0:T(8,128)(2,1)S(1)} %shard_map.48), channel_id=1, replica_groups=mesh['blk'=96,'rep'=2,'slab'=4] {'slab'}, dimensions={0} | all-to-all | bytes 1310720 | tf_op jit(solution)/shard_map/all_to_all | solution.py:332
  37.3 0.7 %shard_map.49 = bf16[640,128]{1,0:T(8,128)(2,1)} custom-call(bf16[4,640,128]{2,1,0:T(8,128)(2,1)S(1)} %all_to_all.11.chunks), custom_call_target="tpu_custom_call" | custom-call | tf_op jit(solution)/shard_map/pallas_call | solution.py:290
Async XLA Ops:
  2.9 13.7 %collective-permute-start = (bf16[2,4,160,128]{3,2,1,0:T(8,128)(2,1)S(1)}, bf16[2,4,160,128]{3,2,1,0:T(8,128)(2,1)S(1)}, u32[]{:S(2)}, u32[]{:S(2)}) collective-permute-start(bf16[2,4,160,128]{3,2,1,0:T(8,128)(2,1)S(1)} %get-tuple-element.15), channel_id=1, source_target_pairs={{0,4},{4,0},{1,5},{5,1},{2,6},{6,2},{3,7},{7,3},{8,12},{12,8},{9,1... | collective-permute-start | bytes 983048 | tf_op jit(solution)/shard_map/ppermute | solution.py:312
  16.8 7.3 %collective-permute-start.1 = (bf16[4,160,128]{2,1,0:T(8,128)(2,1)S(1)}, bf16[4,160,128]{2,1,0:T(8,128)(2,1)S(1)}, u32[]{:S(2)}, u32[]{:S(2)}) collective-permute-start(bf16[4,160,128]{2,1,0:T(8,128)(2,1)S(1)} %get-tuple-element.18), channel_id=1, source_target_pairs={{8,16},{16,8},{24,32},{32,24},{40,48},{48,40},{56,64},{64,56},{72,... | collective-permute-start | bytes 491528 | tf_op jit(solution)/shard_map/ppermute | solution.py:308
  17.4 7.4 %collective-permute-start.2 = (bf16[4,160,128]{2,1,0:T(8,128)(2,1)S(1)}, bf16[4,160,128]{2,1,0:T(8,128)(2,1)S(1)}, u32[]{:S(2)}, u32[]{:S(2)}) collective-permute-start(bf16[4,160,128]{2,1,0:T(8,128)(2,1)S(1)} %get-tuple-element.19), channel_id=1, source_target_pairs={{0,8},{8,0},{16,24},{24,16},{32,40},{40,32},{48,56},{56,48},{64,72... | collective-permute-start | bytes 491528 | tf_op jit(solution)/shard_map/ppermute | solution.py:308
